TPU v7x, 32 devices: a whole 2x2x4 slice. The times are simulated.
32 devices in a mesh: rep: 4 (over y, x), wide: 8 (over z, core).
Axes of the slice: x: 2, y: 2, z: 4, core: 2. Of those that a mesh axis runs over, the one named last changes fastest.
Arguments:
- doc_tokens: bfloat16 [16384, 768], P(('rep', 'wide')), may hold values from -6 to 6
- query_tokens: bfloat16 [8192, 768], P(('rep', 'wide')), may hold values from -6 to 6
- doc_cotangent: bfloat16 [16384, 128], P(('rep', 'wide')), may hold values from -0.017944336 to 0.017944336
- query_cotangent: bfloat16 [8192, 128], P(('rep', 'wide')), may hold values from -0.017944336 to 0.017944336
- retrieved: int32 [16384, 64], P(('rep', 'wide')), may hold values from 0 to 1, as said below
- pos_ids: int32 [256, 4], P(('rep', 'wide')), may hold values from 0 to 7
- pos_count: int32 [256], P(('rep', 'wide')), may hold values from 1 to 4
- w_query: bfloat16 [768, 768], replicated, may hold values from -0.078125 to 0.078125
- w_key: bfloat16 [768, 768], replicated, may hold values from -0.078125 to 0.078125
- carried_content_weights: bfloat16 [768, 768], replicated, may hold values from -0.21875 to 0.21875
- w_out: bfloat16 [768, 768], replicated, may hold values from -0.875 to 0.875
- w_gate: bfloat16 [768, 2048], replicated, may hold values from -0.21875 to 0.21875
- w_up: bfloat16 [768, 2048], replicated, may hold values from -0.21875 to 0.21875
- w_down: bfloat16 [2048, 768], replicated, may hold values from -0.25 to 0.25
- w_proj: bfloat16 [768, 128], replicated, may hold values from -0.21875 to 0.21875
- gain_attn: bfloat16 [768], replicated, may hold values from 0.5 to 1.5
- gain_ffn: bfloat16 [768], replicated, may hold values from 0.5 to 1.5
- gain_final: bfloat16 [768], replicated, may hold values from 0.5 to 1.5
- rel_bias: bfloat16 [32, 12], replicated, may hold values from -4 to 4
Outputs:
- doc_emb: bfloat16 [16384, 128], P(('rep', 'wide'))
- query_emb: bfloat16 [8192, 128], P(('rep', 'wide'))
- doc_grad: bfloat16 [16384, 768], P(('rep', 'wide'))
- query_grad: bfloat16 [8192, 768], P(('rep', 'wide'))
- grad_query: float32 [768, 768], P('wide')
- grad_key: float32 [768, 768], P('wide')
- grad_value: float32 [768, 768], P('wide')
- grad_out: float32 [768, 768], P('wide')
- grad_gate: float32 [768, 2048], P('wide')
- grad_up: float32 [768, 2048], P('wide')
- grad_down: float32 [2048, 768], P('wide')
- grad_proj: float32 [768, 128], P('wide')
- grad_gain_attn: float32 [768], replicated
- grad_gain_ffn: float32 [768], replicated
- grad_gain_final: float32 [768], replicated
- grad_rel_bias: float32 [32, 12], replicated
- loss: float32 [], replicated
- fraction: float32 [], replicated
Inputs may be any that keep to these rules, and one draw needn't show every extreme that they name: Entry (t, q) is 1 where document token t is among the tokens retrieved for query q of the same rep group; queries are numbered within the group. `pos_ids`: the positives of a query are the distinct documents among its first pos_count entries, numbered within its rep group.
All inputs are finite; a program needn't handle non-finite values.
Results may differ from a plain program's by a relative error of at most 0.017.
Values may be sent and summed in bfloat16 or wider, within the bound.
No kernel may reach another device: no remote copies, remote signals or barrier semaphores. Data moves between devices by JAX's collectives and lax.ppermute only.
A program may use at most 192 MiB of HBM per device.

v0:
```python
import math

import jax
import jax.numpy as jnp
import numpy as np
from jax import lax
from jax.sharding import PartitionSpec as P

DL = 512
QUERY_LENGTH = 32


logit_divisor = 0.1
epsilon = 1e-06
peak_logit = lax.Precision.HIGHEST


def bucket_table(length, buckets):
    half = buckets // 2
    exact = half // 2
    context_pos = np.arange(length)[:, None]
    memory_pos = np.arange(length)[None, :]
    relative = memory_pos - context_pos
    base = (relative > 0).astype(np.int64) * half
    distance = np.abs(relative)
    large = exact + (
        np.log(np.maximum(distance, 1) / float(exact)) / np.log(128.0 / exact) * (half - exact)
    ).astype(np.int64)
    large = np.minimum(large, half - 1)
    return (base + np.where(distance < exact, distance, large)).astype(np.int32)


def bucket_onehot(length, buckets):
    table = jnp.asarray(bucket_table(length, buckets))
    numbers = jnp.arange(buckets, dtype=jnp.int32)
    return (table[:, :, None] == numbers[None, None, :]).astype(jnp.float32)


def bias_build(rel_values, length):
    onehot = bucket_onehot(length, rel_values.shape[0])
    return jnp.einsum("ijb,bh->hij", onehot, rel_values, precision=peak_logit)


def bias_grad(d_bias, buckets, length):
    onehot = bucket_onehot(length, buckets)
    return jnp.einsum("ijb,hij->bh", onehot, d_bias, precision=peak_logit)


def rms_forward(values, gain):
    inverse = lax.rsqrt(jnp.mean(values * values, axis=-1, keepdims=True) + epsilon)
    return (values * inverse * gain, inverse)


def rms_back(values, inverse, gain, d_result):
    scaled = values * inverse
    grad_gain = jnp.sum(d_result * scaled, axis=0)
    gained = d_result * gain
    d_values = inverse * (gained - scaled * jnp.mean(gained * scaled, axis=-1, keepdims=True))
    return (d_values, grad_gain)


def gelu_parts(gate):
    inner = 0.7978845608028654 * (gate + 0.044715 * gate * gate * gate)
    tangent = jnp.tanh(inner)
    gelu_value = 0.5 * gate * (1.0 + tangent)
    gelu_slope = 0.5 * (1.0 + tangent) + 0.5 * gate * (
        1.0 - tangent * tangent
    ) * 0.7978845608028654 * (1.0 + 3.0 * 0.044715 * gate * gate)
    return (gelu_value, gelu_slope)


def contract_rows(left, right):
    return jnp.einsum("nd,ne->de", left, right, preferred_element_type=jnp.float32)


def times_transposed(left, right):
    return jnp.einsum("ne,de->nd", left, right, preferred_element_type=jnp.float32)


def layer_forward(tokens, weights, length):
    (
        w_query,
        w_key,
        carried_content_weights,
        w_out,
        w_gate,
        w_up,
        w_down,
        w_proj,
        gain_attn,
        gain_ffn,
        gain_final,
        rel_bias,
    ) = weights
    width = tokens.shape[1]
    heads = rel_bias.shape[1]
    head_size = width // heads
    batch = tokens.shape[0] // length
    flat = tokens.astype(jnp.float32)
    normed_one, inverse_one = rms_forward(flat, gain_attn.astype(jnp.float32))
    normed_one = normed_one.astype(jnp.bfloat16)
    query = (
        jnp.dot(normed_one, w_query, preferred_element_type=jnp.float32)
        .astype(jnp.bfloat16)
        .reshape(batch, length, heads, head_size)
    )
    keys = (
        jnp.dot(normed_one, w_key, preferred_element_type=jnp.float32)
        .astype(jnp.bfloat16)
        .reshape(batch, length, heads, head_size)
    )
    values = (
        jnp.dot(normed_one, carried_content_weights, preferred_element_type=jnp.float32)
        .astype(jnp.bfloat16)
        .reshape(batch, length, heads, head_size)
    )
    bias = bias_build(rel_bias.astype(jnp.float32), length)
    scores = (
        jnp.einsum("bihd,bjhd->bhij", query, keys, preferred_element_type=jnp.float32) + bias[None]
    )
    peak = jnp.max(scores, axis=-1, keepdims=True)
    power_of_e_factor = jnp.exp(scores - peak)
    accumulated_sum = jnp.sum(power_of_e_factor, axis=-1, keepdims=True)
    probs = (power_of_e_factor / accumulated_sum).astype(jnp.bfloat16)
    logsumexp_result = peak + jnp.log(accumulated_sum)
    context = (
        jnp.einsum("bhij,bjhd->bihd", probs, values, preferred_element_type=jnp.float32)
        .astype(jnp.bfloat16)
        .reshape(-1, width)
    )
    hidden = flat + jnp.dot(context, w_out, preferred_element_type=jnp.float32)
    normed_two, inverse_two = rms_forward(hidden, gain_ffn.astype(jnp.float32))
    normed_two = normed_two.astype(jnp.bfloat16)
    gate = jnp.dot(normed_two, w_gate, preferred_element_type=jnp.float32)
    up_values = jnp.dot(normed_two, w_up, preferred_element_type=jnp.float32)
    gelu_value, gelu_slope = gelu_parts(gate)
    act = (gelu_value * up_values).astype(jnp.bfloat16)
    hidden_two = hidden + jnp.dot(act, w_down, preferred_element_type=jnp.float32)
    normed_three, inverse_three = rms_forward(hidden_two, gain_final.astype(jnp.float32))
    normed_three = normed_three.astype(jnp.bfloat16)
    proj = jnp.dot(normed_three, w_proj, preferred_element_type=jnp.float32)
    inverse_len = lax.rsqrt(jnp.sum(proj * proj, axis=-1, keepdims=True) + epsilon)
    emb = (proj * inverse_len).astype(jnp.bfloat16)
    saved = (
        flat,
        normed_one,
        inverse_one,
        query,
        keys,
        values,
        bias,
        logsumexp_result,
        context,
        hidden,
        normed_two,
        inverse_two,
        up_values,
        gelu_value,
        gelu_slope,
        act,
        hidden_two,
        normed_three,
        inverse_three,
        proj,
        inverse_len,
    )
    return (emb, saved)


def back_top(d_emb, saved, weights):
    (
        w_query,
        w_key,
        carried_content_weights,
        w_out,
        w_gate,
        w_up,
        w_down,
        w_proj,
        gain_attn,
        gain_ffn,
        gain_final,
        rel_bias,
    ) = weights
    (
        flat,
        normed_one,
        inverse_one,
        query,
        keys,
        values,
        bias,
        logsumexp_result,
        context,
        hidden,
        normed_two,
        inverse_two,
        up_values,
        gelu_value,
        gelu_slope,
        act,
        hidden_two,
        normed_three,
        inverse_three,
        proj,
        inverse_len,
    ) = saved
    along = jnp.sum(proj * d_emb, axis=-1, keepdims=True)
    d_proj = (
        inverse_len * d_emb - proj * (inverse_len * inverse_len * inverse_len) * along
    ).astype(jnp.bfloat16)
    grad_proj = contract_rows(normed_three, d_proj)
    d_norm_three = times_transposed(d_proj, w_proj)
    d_hidden_two, grad_final = rms_back(
        hidden_two, inverse_three, gain_final.astype(jnp.float32), d_norm_three
    )
    d_branch = d_hidden_two.astype(jnp.bfloat16)
    grad_down = contract_rows(act, d_branch)
    d_act = times_transposed(d_branch, w_down)
    d_gate = (d_act * up_values * gelu_slope).astype(jnp.bfloat16)
    d_up = (d_act * gelu_value).astype(jnp.bfloat16)
    grad_gate = contract_rows(normed_two, d_gate)
    grad_up = contract_rows(normed_two, d_up)
    d_norm_two = times_transposed(d_gate, w_gate) + times_transposed(d_up, w_up)
    d_middle, grad_ffn = rms_back(hidden, inverse_two, gain_ffn.astype(jnp.float32), d_norm_two)
    return (
        d_hidden_two + d_middle,
        (grad_gate, grad_up, grad_down, grad_proj),
        (grad_ffn, grad_final),
    )


def back_attn(d_hidden, saved, weights, length):
    (
        w_query,
        w_key,
        carried_content_weights,
        w_out,
        w_gate,
        w_up,
        w_down,
        w_proj,
        gain_attn,
        gain_ffn,
        gain_final,
        rel_bias,
    ) = weights
    (
        flat,
        normed_one,
        inverse_one,
        query,
        keys,
        values,
        bias,
        logsumexp_result,
        context,
        hidden,
        normed_two,
        inverse_two,
        up_values,
        gelu_value,
        gelu_slope,
        act,
        hidden_two,
        normed_three,
        inverse_three,
        proj,
        inverse_len,
    ) = saved
    width = flat.shape[1]
    d_branch = d_hidden.astype(jnp.bfloat16)
    grad_out = contract_rows(context, d_branch)
    d_context = times_transposed(d_branch, w_out).astype(jnp.bfloat16).reshape(query.shape)
    scores = (
        jnp.einsum("bihd,bjhd->bhij", query, keys, preferred_element_type=jnp.float32) + bias[None]
    )
    probs_full = jnp.exp(scores - logsumexp_result)
    probs = probs_full.astype(jnp.bfloat16)
    d_values = (
        jnp.einsum("bhij,bihd->bjhd", probs, d_context, preferred_element_type=jnp.float32)
        .astype(jnp.bfloat16)
        .reshape(-1, width)
    )
    d_probs = jnp.einsum("bihd,bjhd->bhij", d_context, values, preferred_element_type=jnp.float32)
    d_scores = (
        probs_full * (d_probs - jnp.sum(probs_full * d_probs, axis=-1, keepdims=True))
    ).astype(jnp.bfloat16)
    d_bias = jnp.sum(d_scores.astype(jnp.float32), axis=0)
    d_query = (
        jnp.einsum("bhij,bjhd->bihd", d_scores, keys, preferred_element_type=jnp.float32)
        .astype(jnp.bfloat16)
        .reshape(-1, width)
    )
    d_keys = (
        jnp.einsum("bhij,bihd->bjhd", d_scores, query, preferred_element_type=jnp.float32)
        .astype(jnp.bfloat16)
        .reshape(-1, width)
    )
    grad_query = contract_rows(normed_one, d_query)
    grad_key = contract_rows(normed_one, d_keys)
    grad_value = contract_rows(normed_one, d_values)
    d_norm_one = (
        times_transposed(d_query, w_query)
        + times_transposed(d_keys, w_key)
        + times_transposed(d_values, carried_content_weights)
    )
    d_input, grad_attn = rms_back(flat, inverse_one, gain_attn.astype(jnp.float32), d_norm_one)
    grad_rel = bias_grad(d_bias, rel_bias.shape[0], length)
    return (
        (d_hidden + d_input).astype(jnp.bfloat16),
        (grad_query, grad_key, grad_value, grad_out),
        (grad_attn, grad_rel),
    )


def body(
    doc_tokens,
    query_tokens,
    doc_cotangent,
    query_cotangent,
    retrieved,
    pos_ids,
    pos_count,
    w_query,
    w_key,
    carried_content_weights,
    w_out,
    w_gate,
    w_up,
    w_down,
    w_proj,
    gain_attn,
    gain_ffn,
    gain_final,
    rel_bias,
):
    weights = (
        w_query,
        w_key,
        carried_content_weights,
        w_out,
        w_gate,
        w_up,
        w_down,
        w_proj,
        gain_attn,
        gain_ffn,
        gain_final,
        rel_bias,
    )
    doc_emb, doc_saved = layer_forward(doc_tokens, weights, DL)
    query_emb, query_saved = layer_forward(query_tokens, weights, QUERY_LENGTH)
    every_query = lax.all_gather(query_emb, "wide", axis=0, tiled=True)
    group_count = every_query.shape[0] // QUERY_LENGTH
    score_block_part = math.gcd(group_count, max(1, 512 // QUERY_LENGTH))
    starts = jnp.arange(group_count // score_block_part, dtype=jnp.int32) * score_block_part
    mask_values = retrieved.astype(jnp.float32)
    doc_count = doc_tokens.shape[0] // DL

    def score_parts(doc_one, positive_indicator, start):
        query_block = lax.dynamic_slice_in_dim(
            every_query, start * QUERY_LENGTH, score_block_part * QUERY_LENGTH, 0
        )
        mask_block = lax.dynamic_slice_in_dim(positive_indicator, start, score_block_part, 1)
        pairwise_logits = jnp.einsum(
            "ne,je->nj", query_block, doc_one, preferred_element_type=jnp.float32
        )
        power_of_e_factor = jnp.exp(pairwise_logits / logit_divisor).reshape(
            score_block_part, QUERY_LENGTH, -1
        )
        accumulated_sum = jnp.einsum(
            "mtr,rm->mt", power_of_e_factor, mask_block, precision=peak_logit
        )
        return (query_block, mask_block, power_of_e_factor, accumulated_sum)

    doc_one = doc_emb
    positive_indicator = mask_values

    def mean_block(start):
        parts = score_parts(doc_one, positive_indicator, start)
        return jnp.mean(jnp.log(1.0 + parts[3]), axis=1)

    means = lax.map(mean_block, starts)
    doc_columns = [means.reshape(-1)]
    local_scores = jnp.stack(doc_columns, axis=1)
    local_counts = jnp.transpose(jnp.sum(mask_values.reshape(doc_count, DL, -1), axis=1))
    owner_scores, owner_counts = (
        lax.all_to_all(local_scores, "wide", split_axis=0, concat_axis=1, tiled=True),
        lax.all_to_all(local_counts, "wide", split_axis=0, concat_axis=1, tiled=True),
    )
    numbers = jnp.arange(owner_scores.shape[1], dtype=jnp.int32)
    slots = jnp.arange(pos_ids.shape[1], dtype=jnp.int32)
    matches = (pos_ids[:, :, None] == numbers[None, None, :]) & (
        slots[None, :, None] < pos_count[:, None, None]
    )
    positive_hot = jnp.any(matches, axis=1).astype(jnp.float32)
    peak = jnp.max(owner_scores, axis=1, keepdims=True)
    power_of_e_factor = jnp.exp(owner_scores - peak)
    all_total = jnp.sum(power_of_e_factor, axis=1, keepdims=True)
    positive_total = jnp.sum(positive_hot * power_of_e_factor, axis=1, keepdims=True)
    loss_rows = jnp.log(all_total[:, 0]) - jnp.log(positive_total[:, 0])
    d_owner = power_of_e_factor / all_total - positive_hot * power_of_e_factor / positive_total
    loss_total, positive_hits, positive_docs = lax.psum(
        (jnp.sum(loss_rows), jnp.sum(positive_hot * owner_counts), jnp.sum(positive_hot)),
        ("rep", "wide"),
    )
    query_total = owner_scores.shape[0] * lax.axis_size("rep") * lax.axis_size("wide")
    loss = loss_total / query_total
    fraction = positive_hits / (DL * positive_docs)
    d_local = lax.all_to_all(d_owner, "wide", split_axis=1, concat_axis=0, tiled=True)

    def grad_from_parts(
        carry, start, column, doc_one, query_block, mask_block, exponent_block, accumulated_sum
    ):
        column_block = lax.dynamic_slice_in_dim(column, start, score_block_part, 0)
        d_total = column_block[:, None] / QUERY_LENGTH / (1.0 + accumulated_sum)
        d_similarity = (
            (
                d_total[:, :, None]
                * exponent_block
                * jnp.transpose(mask_block)[:, None, :]
                / logit_divisor
            )
            .astype(jnp.bfloat16)
            .reshape(score_block_part * QUERY_LENGTH, -1)
        )
        carry = carry + jnp.einsum(
            "nj,ne->je", d_similarity, query_block, preferred_element_type=jnp.float32
        )
        return (
            carry,
            jnp.einsum("nj,je->ne", d_similarity, doc_one, preferred_element_type=jnp.float32),
        )

    doc_one = doc_emb
    positive_indicator = mask_values
    column = d_local[:, 0]
    empty = jnp.zeros((DL, every_query.shape[1]), jnp.float32)

    def fresh_step(carry, start):
        query_block, mask_block, exponent_block, accumulated_sum = score_parts(
            doc_one, positive_indicator, start
        )
        return grad_from_parts(
            carry, start, column, doc_one, query_block, mask_block, exponent_block, accumulated_sum
        )

    d_doc_one, d_query_blocks = lax.scan(fresh_step, empty, starts)
    d_query_all = d_query_blocks.reshape(every_query.shape)
    query_part = lax.psum_scatter(d_query_all, "wide", scatter_dimension=0, tiled=True)
    d_doc_emb = doc_cotangent.astype(jnp.float32) + d_doc_one
    d_query_emb = query_cotangent.astype(jnp.float32) + query_part
    doc_hidden, doc_mats, doc_gains = back_top(d_doc_emb, doc_saved, weights)
    query_hidden, query_mats, query_gains = back_top(d_query_emb, query_saved, weights)
    grad_gate = doc_mats[0] + query_mats[0]
    grad_up = doc_mats[1] + query_mats[1]
    grad_down = doc_mats[2] + query_mats[2]
    grad_proj = doc_mats[3] + query_mats[3]
    doc_grad, doc_attn_mats, doc_attn_small = back_attn(doc_hidden, doc_saved, weights, DL)
    query_grad, query_attn_mats, query_attn_small = back_attn(
        query_hidden, query_saved, weights, QUERY_LENGTH
    )
    grad_query = doc_attn_mats[0] + query_attn_mats[0]
    grad_key = doc_attn_mats[1] + query_attn_mats[1]
    grad_value = doc_attn_mats[2] + query_attn_mats[2]
    grad_out = doc_attn_mats[3] + query_attn_mats[3]
    shards = (
        lax.psum_scatter(grad_query, "wide", scatter_dimension=0, tiled=True),
        lax.psum_scatter(grad_key, "wide", scatter_dimension=0, tiled=True),
        lax.psum_scatter(grad_value, "wide", scatter_dimension=0, tiled=True),
        lax.psum_scatter(grad_out, "wide", scatter_dimension=0, tiled=True),
        lax.psum_scatter(grad_gate, "wide", scatter_dimension=0, tiled=True),
        lax.psum_scatter(grad_up, "wide", scatter_dimension=0, tiled=True),
        lax.psum_scatter(grad_down, "wide", scatter_dimension=0, tiled=True),
        lax.psum_scatter(grad_proj, "wide", scatter_dimension=0, tiled=True),
    )
    grad_query, grad_key, grad_value, grad_out, grad_gate, grad_up, grad_down, grad_proj = (
        lax.psum(shards[0].astype(jnp.bfloat16), "rep").astype(jnp.float32),
        lax.psum(shards[1].astype(jnp.bfloat16), "rep").astype(jnp.float32),
        lax.psum(shards[2].astype(jnp.bfloat16), "rep").astype(jnp.float32),
        lax.psum(shards[3].astype(jnp.bfloat16), "rep").astype(jnp.float32),
        lax.psum(shards[4].astype(jnp.bfloat16), "rep").astype(jnp.float32),
        lax.psum(shards[5].astype(jnp.bfloat16), "rep").astype(jnp.float32),
        lax.psum(shards[6].astype(jnp.bfloat16), "rep").astype(jnp.float32),
        lax.psum(shards[7].astype(jnp.bfloat16), "rep").astype(jnp.float32),
    )
    grad_gain_attn, grad_gain_ffn, grad_gain_final, grad_rel_bias = lax.psum(
        (
            doc_attn_small[0] + query_attn_small[0],
            doc_gains[0] + query_gains[0],
            doc_gains[1] + query_gains[1],
            doc_attn_small[1] + query_attn_small[1],
        ),
        ("rep", "wide"),
    )
    return (
        doc_emb,
        query_emb,
        doc_grad,
        query_grad,
        grad_query,
        grad_key,
        grad_value,
        grad_out,
        grad_gate,
        grad_up,
        grad_down,
        grad_proj,
        grad_gain_attn,
        grad_gain_ffn,
        grad_gain_final,
        grad_rel_bias,
        loss,
        fraction,
    )


def solution(mesh):
    return jax.shard_map(
        body,
        mesh=mesh,
        in_specs=(
            P(("rep", "wide"), None),
            P(("rep", "wide"), None),
            P(("rep", "wide"), None),
            P(("rep", "wide"), None),
            P(("rep", "wide"), None),
            P(("rep", "wide"), None),
            P(("rep", "wide")),
            P(),
            P(),
            P(),
            P(),
            P(),
            P(),
            P(),
            P(),
            P(),
            P(),
            P(),
            P(),
        ),
        out_specs=(
            P(("rep", "wide"), None),
            P(("rep", "wide"), None),
            P(("rep", "wide"), None),
            P(("rep", "wide"), None),
            P("wide", None),
            P("wide", None),
            P("wide", None),
            P("wide", None),
            P("wide", None),
            P("wide", None),
            P("wide", None),
            P("wide", None),
            P(),
            P(),
            P(),
            P(),
            P(),
            P(),
        ),
        check_vma=False,
    )
```

profile of v0, /device:TPU:0, one launch (start us, length us, event | category | flops | bytes accessed | tf_op | source)
XLA Modules:
  0.0 795.6 jit_solution(3587701234398163670)
XLA Ops:
  9.1 6.3 all-to-all-start.2
  55.4 12.8 %reshape.374 = bf16[256,768]{1,0:T(8,128)(2,1)} reshape(bf16[8,32,12,64]{3,2,1,0:T(8,128)(2,1)} %copy.174) | data formatting | bytes 786432 | tf_op jit(solution)/shard_map/reshape | solution.py:129
  78.7 16.3 %all_gather.3 = bf16[2048,128]{0,1:T(8,128)(2,1)} all-gather(bf16[256,128]{0,1:T(8,128)(2,1)S(1)} %multiply_convert_fusion.11), channel_id=1, replica_groups=mesh['rep'=4,'wide'=8] {'wide'}, dimensions={0}, use_global_device_ids=true | all-gather | bytes 589824 | tf_op jit(solution)/shard_map/all_gather | solution.py:354
  97.1 9.4 %fusion.14 = f32[512,512,12]{1,2,0:T(8,128)} fusion(s32[512,512]{1,0:T(8,128)} %constant.105.clone, bf16[32,12]{0,1:T(8,128)(2,1)S(1)} %copy-done.130), kind=kOutput, calls=%fused_computation.27 | convolution fusion | flops 209715200 | bytes 13632256 | tf_op jit(solution)/shard_map/ijb,bh->hij/dot_general | solution.py:41
  106.5 17.8 %copy.167 = f32[512,512,12]{0,1,2:T(8,128)} copy(f32[512,512,12]{1,2,0:T(8,128)} %fusion.14) | data formatting | bytes 25165824 | tf_op jit(solution)/shard_map/ijb,bh->hij/dot_general | solution.py:41
  124.2 6.9 fusion.126
  143.0 4.1 multiply_convert_fusion.2
  150.9 37.5 %while.23 = (s32[]{:T(128)}, f32[4,16]{1,0:T(4,128)S(1)}, s32[4]{0:T(128)S(1)}, bf16[2048,128]{1,0:T(8,128)(2,1)}, bf16[512,128]{1,0:T(8,128)(2,1)S(1)}, /*index...) while((s32[]{:T(128)}, f32[4,16]{1,0:T(4,128)S(1)}, ...), condition=%wide.region_14.15_spmd, body=%wide.region_12.14_spmd.sunk | while | flops 70517768 | bytes 2593409 | solution.py:384
  189.7 4.6 all-to-all-start
  195.2 4.6 all-to-all-done
  210.3 52.2 %while.24 = (s32[]{:T(128)}, f32[512,128]{1,0:T(8,128)S(1)}, f32[4,512,128]{2,1,0:T(8,128)}, s32[4]{0:T(128)}, f32[64]{0:T(128)S(1)}, /*index=5*/bf16[2048,128]{...) while((s32[]{:T(128)}, f32[512,128]{1,0:T(8,128)S(1)}, ...), condition=%wide.region_20.21_spmd.clone, body=%wide.region_19.20_spmd.clone.sunk | while | flops 205915168 | bytes 10402323 | solution.py:449
  273.9 6.6 multiply_convert_fusion.1
  289.5 7.3 reduce-scatter.10.cloned.1.call-done
  301.3 5.3 multiply_convert_fusion.3
  317.7 6.9 fusion.49
  335.0 3.7 convolution_add_fusion.5
  339.4 8.0 %multiply_reduce_fusion = (f32[12,512]{1,0:T(8,128)S(1)}, f32[12,512,512]{1,2,0:T(8,128)S(1)}) fusion(f32[12,512,512]{1,2,0:T(8,128)} %copy-done.2, f32[12,512]{1,0:T(8,128)S(1)} %copy-done.101, bf16[512,12,64]{0,2,1:T(8,128)(2,1)} %bitcast.238, bf16[512,12,64]{0,2,1:T(8,128)(2,1)} %bitcast.245), kind=kOutput, calls=%fused_computation.32 | convolution fusion | flops 412084224 | bytes 26787840 | tf_op jit(solution)/shard_map/bihd,bjhd->bhij/dot_general | solution.py:285
  347.4 7.0 multiply_convert_fusion
  363.7 3.8 convolution_add_fusion.7
  368.7 4.8 convolution_convert_fusion.7
  377.3 3.9 convolution_add_fusion.6
  386.2 3.7 convolution_add_fusion.1
  394.6 3.7 convolution_add_fusion.2
  407.9 14.5 %copy.200 = bf16[12,512,512]{2,0,1:T(8,128)(2,1)} copy(bf16[12,512,512]{1,2,0:T(8,128)(2,1)} %copy-done.4) | data formatting | bytes 12582912 | tf_op jit(solution)/shard_map/convert_element_type | solution.py:288
  431.6 8.1 %fusion.63 = f32[32,12]{0,1:T(8,128)} fusion(bf16[12,512,512]{2,0,1:T(8,128)(2,1)} %copy.200, s32[512,512]{1,0:T(8,128)} %constant.105.clone), kind=kOutput, calls=%fused_computation.142 | convolution fusion | flops 209715200 | bytes 7341568 | tf_op jit(solution)/shard_map/ijb,hij->bh/dot_general | solution.py:46
  444.6 17.4 %reduce-scatter.14.cloned.1.call-done = f32[96,768]{1,0:T(8,128)} async-done(((f32[768,768]{1,0:T(8,128)}), f32[96,768]{1,0:T(8,128)}) %reduce-scatter.14.cloned.1.call-update) | async-done | bytes 294928 | tf_op jit(solution)/shard_map/reduce_scatter | solution.py:470
  463.6 69.5 %reduce-scatter.24.cloned.1.call-done = f32[256,768]{1,0:T(8,128)} async-done(((f32[2048,768]{1,0:T(8,128)}), f32[256,768]{1,0:T(8,128)}) %reduce-scatter.24.cloned.1.call-update) | async-done | bytes 786448 | tf_op jit(solution)/shard_map/reduce_scatter | solution.py:475
  535.1 68.5 %reduce-scatter.22.cloned.1.call-done = f32[96,2048]{1,0:T(8,128)} async-done(((f32[768,2048]{1,0:T(8,128)}), f32[96,2048]{1,0:T(8,128)}) %reduce-scatter.22.cloned.1.call-update) | async-done | bytes 786448 | tf_op jit(solution)/shard_map/reduce_scatter | solution.py:474
  605.5 68.6 %reduce-scatter.20.cloned.1.call-done = f32[96,2048]{1,0:T(8,128)} async-done(((f32[768,2048]{1,0:T(8,128)}), f32[96,2048]{1,0:T(8,128)}) %reduce-scatter.20.cloned.1.call-update) | async-done | bytes 786448 | tf_op jit(solution)/shard_map/reduce_scatter | solution.py:473
  687.7 38.8 %all-reduce = (f32[768]{0:T(1024)}, f32[768]{0:T(1024)}, f32[768]{0:T(1024)}, f32[32,12]{0,1:T(8,128)}, f32[]{:T(128)}, /*index=5*/f32[]{:T(128)}, f32[]{:T(128)}) all-reduce(f32[768]{0:T(1024)S(1)} %add.334, f32[768]{0:T(1024)S(1)} %add.335, f32[768]{0:T(1024)S(1)} %copy-done.134, ...), channel_id=1, replica_groups=mesh['rep'=4,'wide'=8] {'rep','wide'}, use_global_device_ids=true, to_apply=%region_50.51 | all-reduce | flops 2691 | bytes 21528 | tf_op jit(solution)/shard_map/psum | solution.py:488
  731.4 16.9 %psum.112 = bf16[96,128]{1,0:T(8,128)(2,1)S(1)} all-reduce(bf16[96,128]{1,0:T(8,128)(2,1)S(1)} %convert_element_type.347), channel_id=1, replica_groups=mesh['rep'=4,'wide'=8] {'rep'}, use_global_device_ids=true, to_apply=%region_47.48 | all-reduce | flops 12288 | bytes 49152 | tf_op jit(solution)/shard_map/psum | solution.py:486
  749.0 26.7 %all-reduce.4.cloned.1.call-done = (bf16[96,768]{1,0:T(8,128)(2,1)}, bf16[96,768]{1,0:T(8,128)(2,1)}, bf16[96,768]{1,0:T(8,128)(2,1)}, bf16[96,768]{1,0:T(8,128)...) async-done(((bf16[96,768]{1,0:T(8,128)(2,1)}, bf16[96,768]{1,0:T(8,128)(2,1)}, bf16[96,768]{1,0:T(8,128)(2,1)}, ...) | async-done | bytes 1769488 | tf_op jit(solution)/shard_map/psum | solution.py:479
  (585 shorter events, 277.6 us)
Async XLA Ops:
  7.2 64.5 %copy-start = (bf16[768,2048]{1,0:T(8,128)(2,1)S(1)}, bf16[768,2048]{1,0:T(8,128)(2,1)}, u32[]{:S(2)}) copy-start(bf16[768,2048]{1,0:T(8,128)(2,1)} %param.39) | copy-start | bytes 9437188
  7.2 16.4 %copy-start.14 = (bf16[256,768]{1,0:T(8,128)(2,1)S(1)}, bf16[256,768]{1,0:T(8,128)(2,1)}, u32[]{:S(2)}) copy-start(bf16[256,768]{1,0:T(8,128)(2,1)} %param.28) | copy-start | bytes 1179652
  9.1 180.7 %all-to-all-start.2 = ((f32[8,8,1]{1,2,0:T(1,128)}), f32[8,8,1]{1,2,0:T(1,128)}, u32[]{:S(2)}, u32[]{:S(2)}) async-start(f32[8,8,1]{1,2,0:T(1,128)} %bitcast.45), calls=%async_computation.11 | async-start | bytes 8192 | tf_op jit(solution)/shard_map/all_to_all | solution.py:390
  18.8 9.6 %copy-start.117 = (f32[256]{0:T(256)}, f32[256]{0:T(256)S(1)}, u32[]{:S(2)}) copy-start(f32[256]{0:T(256)S(1)} %add_rsqrt_fusion.7) | copy-start | bytes 3076
  20.1 9.5 %copy-start.112 = (f32[512]{0:T(512)}, f32[512]{0:T(512)S(1)}, u32[]{:S(2)}) copy-start(f32[512]{0:T(512)S(1)} %add_rsqrt_fusion.3) | copy-start | bytes 6148
  32.7 106.7 %copy-start.108 = (f32[768]{0:T(1024)}, f32[768]{0:T(1024)S(1)}, u32[]{:S(2)}) copy-start(f32[768]{0:T(1024)S(1)} %convert_element_type.279) | copy-start | bytes 9220
  76.2 20.9 %copy-start.130 = (bf16[32,12]{0,1:T(8,128)(2,1)S(1)}, bf16[32,12]{0,1:T(8,128)(2,1)}, u32[]{:S(2)}) copy-start(bf16[32,12]{0,1:T(8,128)(2,1)} %param.45) | copy-start | bytes 2308
  76.2 30.3 %copy-start.122 = (f32[256]{0:T(256)}, f32[256]{0:T(256)S(1)}, u32[]{:S(2)}) copy-start(f32[256]{0:T(256)S(1)} %add_rsqrt_fusion.5) | copy-start | bytes 3076
  78.0 28.5 %copy-start.137 = (f32[256]{0:T(256)}, f32[256]{0:T(256)S(1)}, u32[]{:S(2)}) copy-start(f32[256]{0:T(256)S(1)} %get-tuple-element.320) | copy-start | bytes 3076
  150.5 43.9 %copy-start.140 = (s32[8,4]{0,1:T(4,128)S(1)}, s32[8,4]{0,1:T(4,128)}, u32[]{:S(2)}) copy-start(s32[8,4]{0,1:T(4,128)} %param.32) | copy-start | bytes 388
  189.7 10.1 %all-to-all-start = ((f32[8,8,1]{1,2,0:T(1,128)}), f32[8,8,1]{1,2,0:T(1,128)S(1)}, u32[]{:S(2)}, u32[]{:S(2)}) async-start(f32[8,8,1]{1,2,0:T(1,128)} %bitcast.16), calls=%async_computation | async-start | bytes 8192 | tf_op jit(solution)/shard_map/all_to_all | solution.py:389
  201.5 8.7 %all-to-all-start.1 = ((f32[8,8,1]{0,2,1:T(1,128)}), f32[8,8,1]{0,2,1:T(1,128)S(1)}, u32[]{:S(2)}, u32[]{:S(2)}) async-start(f32[8,8,1]{0,2,1:T(1,128)} %copy.181), calls=%async_computation.1 | async-start | bytes 8192 | tf_op jit(solution)/shard_map/all_to_all | solution.py:411
  204.8 92.0 %reduce-scatter.10.cloned.1.call-start = ((), (), s32[]{:S(2)}) async-start(), calls=%async_computation.12 | async-start | bytes 1179648 | tf_op jit(solution)/shard_map/reduce_scatter | solution.py:451
  265.2 174.5 %reduce-scatter.18.cloned.1.call-start = ((), (), s32[]{:S(2)}) async-start(), calls=%async_computation.16 | async-start | bytes 2654208 | tf_op jit(solution)/shard_map/reduce_scatter | solution.py:472
  271.7 14.0 %copy-start.19 = (f32[512,768]{1,0:T(8,128)}, f32[512,768]{1,0:T(8,128)S(1)}, u32[]{:S(2)}) copy-start(f32[512,768]{1,0:T(8,128)S(1)} %subtract_multiply_fusion) | copy-start | bytes 4718596
  287.3 9.4 %copy-start.75 = (f32[256,128]{0,1:T(8,128)S(1)}, f32[256,128]{0,1:T(8,128)}, u32[]{:S(2)}) copy-start(f32[256,128]{0,1:T(8,128)} %copy-done.74) | copy-start | bytes 393220
  287.3 9.4 %copy-start.97 = (bf16[256,128]{0,1:T(8,128)(2,1)S(1)}, bf16[256,128]{0,1:T(8,128)(2,1)}, u32[]{:S(2)}) copy-start(bf16[256,128]{0,1:T(8,128)(2,1)} %copy.189) | copy-start | bytes 196612
  287.3 11.4 %copy-start.73 = (bf16[768,128]{1,0:T(8,128)(2,1)S(1)}, bf16[768,128]{1,0:T(8,128)(2,1)}, u32[]{:S(2)}) copy-start(bf16[768,128]{1,0:T(8,128)(2,1)} %param.41) | copy-start | bytes 589828
  301.3 8.8 %copy-start.31 = (f32[256,768]{1,0:T(8,128)}, f32[256,768]{1,0:T(8,128)S(1)}, u32[]{:S(2)}) copy-start(f32[256,768]{1,0:T(8,128)S(1)} %subtract_multiply_fusion.1) | copy-start | bytes 2359300
  311.8 16.1 %copy-start.26 = (f32[256,768]{1,0:T(8,128)}, f32[256,768]{1,0:T(8,128)S(1)}, u32[]{:S(2)}) copy-start(f32[256,768]{1,0:T(8,128)S(1)} %multiply_add_fusion.3) | copy-start | bytes 2359300
  313.7 127.6 %reduce-scatter.16.cloned.1.call-start = ((), (), s32[]{:S(2)}) async-start(), calls=%async_computation.15 | async-start | bytes 2654208 | tf_op jit(solution)/shard_map/reduce_scatter | solution.py:471
  338.7 104.3 %reduce-scatter.12.cloned.1.call-start = ((), (), s32[]{:S(2)}) async-start(), calls=%async_computation.13 | async-start | bytes 2654208 | tf_op jit(solution)/shard_map/reduce_scatter | solution.py:469
  367.6 94.4 %reduce-scatter.14.cloned.1.call-start = ((), (), s32[]{:S(2)}) async-start(), calls=%async_computation.14 | async-start | bytes 2654208 | tf_op jit(solution)/shard_map/reduce_scatter | solution.py:470
  381.2 151.9 %reduce-scatter.24.cloned.1.call-start = ((), (), s32[]{:S(2)}) async-start(), calls=%async_computation.19 | async-start | bytes 7077888 | tf_op jit(solution)/shard_map/reduce_scatter | solution.py:475
  390.0 213.6 %reduce-scatter.22.cloned.1.call-start = ((), (), s32[]{:S(2)}) async-start(), calls=%async_computation.18 | async-start | bytes 7077888 | tf_op jit(solution)/shard_map/reduce_scatter | solution.py:474
  398.4 275.7 %reduce-scatter.20.cloned.1.call-start = ((), (), s32[]{:S(2)}) async-start(), calls=%async_computation.17 | async-start | bytes 7077888 | tf_op jit(solution)/shard_map/reduce_scatter | solution.py:473
  405.7 324.9 %reduce-scatter.26.cloned.1.call-start = ((), (), s32[]{:S(2)}) async-start(), calls=%async_computation.20 | async-start | bytes 442368 | tf_op jit(solution)/shard_map/reduce_scatter | solution.py:476
  407.9 14.6 %copy-start.44 = (bf16[12,64,512]{2,1,0:T(8,128)(2,1)S(1)}, bf16[12,64,512]{2,1,0:T(8,128)(2,1)}, u32[]{:S(2)}) copy-start(bf16[12,64,512]{2,1,0:T(8,128)(2,1)} %copy-done.43) | copy-start | bytes 2359300
  431.5 344.2 %all-reduce.4.cloned.1.call-start = ((), (), s32[]{:S(2)}) async-start(), calls=%async_computation.21 | async-start | bytes 3538944 | tf_op jit(solution)/shard_map/psum | solution.py:479
  535.1 141.0 %copy-start.18 = (f32[512,768]{1,0:T(8,128)S(1)}, f32[512,768]{1,0:T(8,128)}, u32[]{:S(2)}) copy-start(f32[512,768]{1,0:T(8,128)} %copy-done.16) | copy-start | bytes 4718596
  685.8 42.7 %copy-start.27 = (f32[256,768]{1,0:T(8,128)S(1)}, f32[256,768]{1,0:T(8,128)}, u32[]{:S(2)}) copy-start(f32[256,768]{1,0:T(8,128)} %copy-done.26) | copy-start | bytes 2359300
  775.7 9.7 %copy-start.102 = (bf16[256,768]{1,0:T(8,128)(2,1)S(1)}, bf16[256,768]{1,0:T(8,128)(2,1)}, u32[]{:S(2)}) copy-start(bf16[256,768]{1,0:T(8,128)(2,1)} %get-tuple-element.308) | copy-start | bytes 1179652
  (147 other events, 432.3 us)
Sparse Core Ops, SparseCore 0:
  265.3 31.4 reduce-scatter.9
  313.9 34.5 reduce-scatter.17
  350.8 35.5 reduce-scatter.15
  388.6 35.4 reduce-scatter.11
  426.2 35.6 reduce-scatter.13
  464.1 68.9 reduce-scatter.23
  535.4 68.1 reduce-scatter.21
  605.9 68.1 reduce-scatter.19
  676.4 28.9 reduce-scatter.25
  710.8 64.8 all-reduce.3
where the time goes:
time: 803 us; the launch traced here: 796 us
  waiting for transfers between devices  265 us (33%)
  matrix products  197 us (25%)
  local copies, waits for them, and re-layouts  138 us (17%)
  blocking collectives  72 us (9%)
  other arithmetic  66.6 us (8%)
  loops' own time  21.1 us (3%)
  between operations  20.3 us (3%)
  starting transfers between devices  15.6 us (2%)
    reduce_scatter x1, waiting for transfers between devices, body(): lax.psum_scatter(grad_down, 'wide', scatter_dimension=0, tiled=True)  69.5 us
    reduce_scatter x1, waiting for transfers between devices, body(): lax.psum_scatter(grad_gate, 'wide', scatter_dimension=0, tiled=True)  68.6 us
    reduce_scatter x1, waiting for transfers between devices, body(): lax.psum_scatter(grad_up, 'wide', scatter_dimension=0, tiled=True)  68.5 us
    dot_general x16, matrix products, contract_rows(): jnp.einsum('nd,ne->de', left, right, preferred_element_type=jnp.float32)  45.9 us
    psum x1, blocking collectives, body(): lax.psum((doc_attn_small[0] + query_attn_small[0], doc_gains[0] + query_g...  38.8 us
    dot_general x16, matrix products, times_transposed(): jnp.einsum('ne,de->nd', left, right, preferred_element_type=jnp.float32)  37.9 us
    unnamed x304, local copies, waits for them, and re-layouts  26.8 us
    psum x1, waiting for transfers between devices, body(): lax.psum(shards[0].astype(jnp.bfloat16), 'rep').astype(jnp.float32)  26.7 us
  transfers between devices with their start and end apart: 13, of which 8 were waited for; matrix products, arithmetic and copies ran while one was open for 38% of the time, Pallas kernels for 0%

commit v1 on v0

v1 whole, which is shorter than its diff:
```python
import functools

import jax
import jax.numpy as jnp
import numpy as np
from jax import lax
from jax.experimental import pallas as pl
from jax.experimental.pallas import tpu as pltpu
from jax.sharding import PartitionSpec as P

DL = 512
QUERY_LENGTH = 32
EPS = 1e-06
SCALE = 10.0
BF = jnp.bfloat16
F = jnp.float32
TABLE = 1024
SHIFT = 384
VMEM_LIMIT = 60 * 1024 * 1024

SAVED = (
    "n1", "q", "k", "v", "p", "li", "ctx", "hid", "n2", "gv", "us", "act", "h2", "n3", "proj", "emb",
)

SM = pl.BlockSpec(memory_space=pltpu.SMEM)
ANY = pl.BlockSpec(memory_space=pl.ANY)
VM = pl.BlockSpec(memory_space=pltpu.VMEM)


def mm(a, b):
    return jnp.dot(a, b, preferred_element_type=F)


def mm_nt(a, b):
    return lax.dot_general(a, b, (((1,), (1,)), ((), ())), preferred_element_type=F)


def mm_tn(a, b):
    return lax.dot_general(a, b, (((0,), (0,)), ((), ())), preferred_element_type=F)


def bucket_hot(buckets):
    half = buckets // 2
    exact = half // 2
    column = np.arange(TABLE)
    relative = np.where(column < TABLE - 128, column, column - TABLE) - SHIFT
    base = (relative > 0).astype(np.int64) * half
    distance = np.abs(relative)
    large = exact + (
        np.log(np.maximum(distance, 1) / float(exact)) / np.log(128.0 / exact) * (half - exact)
    ).astype(np.int64)
    large = np.minimum(large, half - 1)
    number = base + np.where(distance < exact, distance, large)
    return (np.arange(buckets)[:, None] == number[None, :]).astype(np.float32)


def query_hot(queries):
    tokens = np.arange(queries * QUERY_LENGTH)
    return (np.arange(queries)[:, None] == tokens[None, :] // QUERY_LENGTH).astype(np.float32)


def cost(flops, moved):
    large = flops > 1e8
    return pl.CostEstimate(flops=int(1e12 if large else 1), bytes_accessed=1, transcendentals=0)


def sds(shape, dtype):
    return jax.ShapeDtypeStruct(shape, dtype)


def rows_loop(count, block, fn):
    def step(i, carry):
        fn(pl.ds(pl.multiple_of(i * block, block), block))
        return carry

    lax.fori_loop(0, count // block, step, 0)


def half_masks():
    lane = lax.broadcasted_iota(jnp.int32, (1, 128), 1)
    low = (lane < 64).astype(F)
    high = 1.0 - low
    one_low = (lane == 0).astype(F)
    one_high = (lane == 64).astype(F)
    return low, high, one_low, one_high


def rms(values):
    return lax.rsqrt(jnp.mean(values * values, axis=-1, keepdims=True) + EPS)


def rms_back(values, gain, d_result):
    inverse = rms(values)
    scaled = values * inverse
    grad_gain = jnp.sum(d_result * scaled, axis=0, keepdims=True)
    gained = d_result * gain
    d_values = inverse * (gained - scaled * jnp.mean(gained * scaled, axis=-1, keepdims=True))
    return d_values, grad_gain


def gelu_parts(gate):
    square = gate * gate
    tangent = jnp.tanh(gate * (0.7978845608028654 + (0.7978845608028654 * 0.044715) * square))
    half_plus = 0.5 + 0.5 * tangent
    value = gate * half_plus
    slope = half_plus + 0.5 * gate * (1.0 - tangent * tangent) * (
        0.7978845608028654 + (3.0 * 0.7978845608028654 * 0.044715) * square
    )
    return value, slope


def fwd_kernel(
    seq,
    heads,
    n_after,
    tok, gains, rel, hot, wq_h, wk_h, wv_h, wo_h, wg_h, wu_h, wd_h, wp_h,
    *refs,
):
    (
    n1_h, q_h, k_h, v_h, p_h, li_h, ctx_h, hid_h, n2_h, gv_h, us_h, act_h, h2_h, n3_h, proj_h, emb,
    wq, wk, wv, wo, wg, wu, wd, wp,
    n1, q, k, v, p, li, ctx, hid, n2, gv, us, act, h2, n3, proj,
    tbl, bs, sem_in, sem_out,
    ) = refs[n_after:]
    count = tok.shape[0]
    loads = [
        pltpu.make_async_copy(src, dst, sem_in.at[i])
        for i, (src, dst) in enumerate(
            zip((wq_h, wk_h, wv_h, wo_h, wg_h, wu_h, wd_h, wp_h), (wq, wk, wv, wo, wg, wu, wd, wp))
        )
    ]
    for copy in loads:
        copy.start()
    outs = {}

    def push(i, src, dst):
        outs[i] = pltpu.make_async_copy(src, dst, sem_out.at[i])
        outs[i].start()

    gain_a = gains[0:1, :]
    gain_f = gains[1:2, :]
    gain_l = gains[2:3, :]

    def norm_one(rows):
        x = tok[rows, :].astype(F)
        n1[rows, :] = (x * rms(x) * gain_a).astype(BF)

    rows_loop(count, 128, norm_one)
    push(0, n1, n1_h)
    tbl[0:heads, :] = mm(rel[...], hot[...])
    for i, (w, r, r_h) in enumerate(((wq, q, q_h), (wk, k, k_h), (wv, v, v_h))):
        loads[i].wait()
        r[...] = mm(n1[...], w[...]).astype(BF)
        push(1 + i, r, r_h)

    low, high, one_low, one_high = half_masks()
    is_low = low > 0.5

    def pair(index, carry):
        lanes = pl.ds(pl.multiple_of(index * 128, 128), 128)
        q2 = q[:, lanes]
        k2 = k[:, lanes]
        v2 = v[:, lanes]
        parts = []
        for e, (keep, one) in enumerate(((low, one_high), (high, one_low))):
            head = 2 * index + e
            km = k2 * keep.astype(BF)
            vm = v2 * keep.astype(BF) + one.astype(BF)
            row = jnp.broadcast_to(tbl[pl.ds(head, 1), :], (128, TABLE))
            base = pltpu.roll(row, 0, 1, stride=1, stride_axis=0)
            if seq == DL:
                bs[...] = base
            else:
                ri = lax.broadcasted_iota(jnp.int32, (128, 128), 0) // seq
                ci = lax.broadcasted_iota(jnp.int32, (128, 128), 1) // seq
                bs[:, 0:128] = jnp.where(ri == ci, base[:, SHIFT : SHIFT + 128], -1e30)
            blocks = []
            for i in range(count // 128):
                qb = q2[128 * i : 128 * i + 128]
                if seq == DL:
                    kb, vb = km, vm
                    bias = bs[:, SHIFT - 128 * i : SHIFT - 128 * i + DL]
                else:
                    kb = km[128 * i : 128 * i + 128]
                    vb = vm[128 * i : 128 * i + 128]
                    bias = bs[:, 0:128]
                scores = mm_nt(qb, kb) + bias
                peak = jnp.max(scores, axis=1, keepdims=True)
                pb = jnp.exp(scores - peak).astype(BF)
                p[head, 128 * i : 128 * i + 128, :] = pb
                o = mm(pb, vb)
                total = o[:, 64:65] if e == 0 else o[:, 0:1]
                blocks.append((o, 1.0 / total))
            parts.append(blocks)
        for i in range(count // 128):
            (o0, i0), (o1, i1) = parts[0][i], parts[1][i]
            inv = jnp.where(is_low, i0, i1)
            li[128 * i : 128 * i + 128, lanes] = inv
            ctx[128 * i : 128 * i + 128, lanes] = (jnp.where(is_low, o0, o1) * inv).astype(BF)
        return carry

    lax.fori_loop(0, heads // 2, pair, 0)
    push(4, p, p_h)
    push(5, li, li_h)
    push(6, ctx, ctx_h)

    loads[3].wait()

    def middle(rows):
        h = tok[rows, :].astype(F) + mm(ctx[rows, :], wo[...])
        hid[rows, :] = h
        h2[rows, :] = h
        n2[rows, :] = (h * rms(h) * gain_f).astype(BF)

    rows_loop(count, 256, middle)
    push(7, hid, hid_h)
    push(8, n2, n2_h)
    loads[4].wait()
    loads[5].wait()
    loads[6].wait()

    def ffn(t, carry):
        cols = pl.ds(pl.multiple_of(t * 512, 512), 512)
        for b in range(count // 256):
            rows = slice(256 * b, 256 * b + 256)
            gate = mm(n2[rows, :], wg[:, cols])
            up = mm(n2[rows, :], wu[:, cols])
            value, slope = gelu_parts(gate)
            a = (value * up).astype(BF)
            gv[rows, cols] = value.astype(BF)
            us[rows, cols] = (up * slope).astype(BF)
            act[rows, cols] = a
            h2[rows, :] += mm(a, wd[cols, :])
        return carry

    lax.fori_loop(0, wg.shape[1] // 512, ffn, 0)
    push(9, gv, gv_h)
    push(10, us, us_h)
    push(11, act, act_h)
    loads[7].wait()

    def top(rows):
        h = h2[rows, :]
        n = (h * rms(h) * gain_l).astype(BF)
        n3[rows, :] = n
        pr = mm(n, wp[...])
        proj[rows, :] = pr
        emb[rows, :] = (pr * lax.rsqrt(jnp.sum(pr * pr, axis=-1, keepdims=True) + EPS)).astype(BF)

    rows_loop(count, 256, top)
    push(12, h2, h2_h)
    push(13, n3, n3_h)
    push(14, proj, proj_h)
    for copy in outs.values():
        copy.wait()


def layer_forward(tokens, weights, gains, rel, hot, seq, after=()):
    count, width = tokens.shape
    wq, wk, wv, wo, wg, wu, wd, wp = weights
    hidden = wg.shape[1]
    emb = wp.shape[1]
    heads = rel.shape[0]
    keys = DL if seq == DL else 128
    saved = (
        sds((count, width), BF),
        sds((count, width), BF),
        sds((count, width), BF),
        sds((count, width), BF),
        sds((heads, count, keys), BF),
        sds((count, width), F),
        sds((count, width), BF),
        sds((count, width), F),
        sds((count, width), BF),
        sds((count, hidden), BF),
        sds((count, hidden), BF),
        sds((count, hidden), BF),
        sds((count, width), F),
        sds((count, width), BF),
        sds((count, emb), F),
    )
    outs = pl.pallas_call(
        functools.partial(fwd_kernel, seq, heads, len(after)),
        out_shape=saved + (sds((count, emb), BF),),
        in_specs=[VM] * 4 + [ANY] * (8 + len(after)),
        out_specs=[ANY] * 15 + [VM],
        scratch_shapes=[pltpu.VMEM(w.shape, BF) for w in weights]
        + [pltpu.VMEM(s.shape, s.dtype) for s in saved]
        + [
            pltpu.VMEM((16, TABLE), F),
            pltpu.VMEM((128, TABLE), F),
            pltpu.SemaphoreType.DMA((8,)),
            pltpu.SemaphoreType.DMA((15,)),
        ],
        compiler_params=pltpu.CompilerParams(vmem_limit_bytes=VMEM_LIMIT),
        cost_estimate=cost(count * 14e6, 40e6),
        name="layer_forward_%d" % seq,
    )(tokens, gains, rel, hot, *weights, *after)
    return dict(zip(SAVED, outs))


def each_block(arrays, block, fn):
    first = 0
    for array in arrays:
        number = array.shape[0] // block
        if number == 1:
            fn(first, array[...])
        else:

            def step(i, carry, array=array, first=first):
                fn(first + i, array[pl.ds(pl.multiple_of(i * block, block), block), :])
                return carry

            lax.fori_loop(0, number, step, 0)
        first += number


def query_sims_kernel(n_arrays, number, qemb, mask, ids, used, cot, *refs):
    docs = refs[:n_arrays]
    coef, d_emb, parts, es, total, counts = refs[n_arrays:]
    n_docs = mask.shape[0]
    tokens = qemb.shape[0]
    queries = tokens // QUERY_LENGTH
    lane = lax.broadcasted_iota(jnp.int32, (tokens, 128), 1)
    lane_q = lax.broadcasted_iota(jnp.int32, (queries, 128), 1)
    total[...] = jnp.zeros_like(total)
    counts[...] = jnp.zeros_like(counts)

    def forward(slot, rows):
        d = number[slot]
        m = mask[d]
        wide = jnp.broadcast_to(m[:, None, :], (queries, QUERY_LENGTH, DL)).reshape(tokens, DL)
        e = jnp.exp(mm_nt(qemb[...], rows) * SCALE) * wide
        es[slot] = e
        total[...] = jnp.where(lane == d, jnp.sum(e, axis=1, keepdims=True), total[...])
        counts[...] = jnp.where(lane_q == d, jnp.sum(m, axis=1, keepdims=True), counts[...])

    each_block(docs, DL, forward)
    inside = lane_q < n_docs
    z = jnp.sum(jnp.log(1.0 + total[...]).reshape(queries, QUERY_LENGTH, 128), axis=1)
    z = z * (1.0 / QUERY_LENGTH)
    hot = jnp.zeros((queries, 128), F)
    for s in range(ids.shape[1]):
        here = (ids[:, s : s + 1] == lane_q) & (used[...] > s)
        hot = jnp.where(here, 1.0, hot)
    peak = jnp.max(jnp.where(inside, z, -1e30), axis=1, keepdims=True)
    power = jnp.where(inside, jnp.exp(jnp.where(inside, z - peak, 0.0)), 0.0)
    whole = jnp.sum(power, axis=1, keepdims=True)
    positive = jnp.sum(hot * power, axis=1, keepdims=True)
    loss = jnp.sum(jnp.log(whole) - jnp.log(positive))
    hits = jnp.sum(hot * counts[...])
    found = jnp.sum(hot)
    lane_p = lax.broadcasted_iota(jnp.int32, (8, 128), 1)
    parts[...] = jnp.where(
        lane_p == 0, loss, jnp.where(lane_p == 1, hits, jnp.where(lane_p == 2, found, 0.0))
    )
    d_z = power / whole - hot * power / positive
    d_wide = jnp.broadcast_to(d_z[:, None, :], (queries, QUERY_LENGTH, 128)).reshape(tokens, 128)
    c = d_wide * (SCALE / QUERY_LENGTH) / (1.0 + total[...])
    coef[...] = jnp.transpose(c)[0:n_docs, :]
    d_emb[...] = cot[...].astype(F)

    def backward(slot, rows):
        column = jnp.sum(jnp.where(lane == number[slot], c, 0.0), axis=1, keepdims=True)
        d_emb[...] += mm((es[slot] * column).astype(BF), rows)

    each_block(docs, DL, backward)


def query_sims(number, qemb, docs, mask, ids, used, cot):
    n_docs = mask.shape[0]
    tokens, emb = qemb.shape
    queries = tokens // QUERY_LENGTH
    return pl.pallas_call(
        functools.partial(query_sims_kernel, len(docs)),
        out_shape=(sds((n_docs, tokens), F), sds((tokens, emb), F), sds((8, 128), F)),
        in_specs=[SM] + [VM] * (5 + len(docs)),
        out_specs=[VM] * 3,
        scratch_shapes=[
            pltpu.VMEM((n_docs, tokens, DL), F),
            pltpu.VMEM((tokens, 128), F),
            pltpu.VMEM((queries, 128), F),
        ],
        compiler_params=pltpu.CompilerParams(vmem_limit_bytes=VMEM_LIMIT),
        cost_estimate=cost(n_docs * 67e6 * 10, n_docs * 1e6),
        name="query_sims",
    )(number, qemb, mask, ids, used, cot, *docs)


def top_rows(d_emb, proj, h2, gain, wp):
    inv = lax.rsqrt(jnp.sum(proj * proj, axis=-1, keepdims=True) + EPS)
    along = jnp.sum(proj * d_emb, axis=-1, keepdims=True)
    d_proj = (inv * d_emb - proj * (inv * inv * inv) * along).astype(BF)
    d_h2, grad_gain = rms_back(h2, gain, mm_nt(d_proj, wp))
    return d_proj, d_h2, grad_gain


def query_back_kernel(
    d_emb, proj, gains,
    h2_h, hid_h, gv_h, us_h, wp_h, wd_h, wg_h, wu_h, after,
    d_proj, d_ffn, d_gate_h, d_up_h, d_hid, g_gains,
    h2, hid, gv, us, wp, wd, wg, wu, d_gate, d_up, d_h2, d_n2, sem_in, sem_out,
):
    count = d_emb.shape[0]
    loads = [
        pltpu.make_async_copy(src, dst, sem_in.at[i])
        for i, (src, dst) in enumerate(
            zip((h2_h, wp_h, wd_h, us_h, gv_h, wg_h, wu_h, hid_h), (h2, wp, wd, us, gv, wg, wu, hid))
        )
    ]
    for copy in loads:
        copy.start()
    gain_f = gains[1:2, :]
    gain_l = gains[2:3, :]
    loads[0].wait()
    loads[1].wait()
    dp, dh, gg = top_rows(d_emb[...], proj[...], h2[...], gain_l, wp[...])
    d_proj[...] = dp
    d_h2[...] = dh
    g_gains[...] = jnp.zeros_like(g_gains)
    g_gains[1:2, :] = gg
    d_ffn[...] = dh.astype(BF)
    d_n2[...] = jnp.zeros_like(d_n2)
    for i in range(2, 7):
        loads[i].wait()

    def ffn(t, carry):
        cols = pl.ds(pl.multiple_of(t * 512, 512), 512)
        d_act = mm_nt(d_ffn[...], wd[cols, :])
        dg = (d_act * us[:, cols].astype(F)).astype(BF)
        du = (d_act * gv[:, cols].astype(F)).astype(BF)
        d_gate[:, cols] = dg
        d_up[:, cols] = du
        d_n2[...] += mm_nt(dg, wg[:, cols]) + mm_nt(du, wu[:, cols])
        return carry

    lax.fori_loop(0, wg.shape[1] // 512, ffn, 0)
    out_gate = pltpu.make_async_copy(d_gate, d_gate_h, sem_out.at[0])
    out_up = pltpu.make_async_copy(d_up, d_up_h, sem_out.at[1])
    out_gate.start()
    out_up.start()
    loads[7].wait()
    dm, gg = rms_back(hid[...], gain_f, d_n2[...])
    d_hid[...] = d_h2[...] + dm
    g_gains[0:1, :] = gg
    out_gate.wait()
    out_up.wait()


def query_back(d_emb, saved, weights, gains, after):
    wq, wk, wv, wo, wg, wu, wd, wp = weights
    count, emb = d_emb.shape
    width, hidden = wg.shape
    return pl.pallas_call(
        query_back_kernel,
        out_shape=(
            sds((count, emb), BF),
            sds((count, width), BF),
            sds((count, hidden), BF),
            sds((count, hidden), BF),
            sds((count, width), F),
            sds((8, width), F),
        ),
        in_specs=[VM] * 3 + [ANY] * 9,
        out_specs=[VM, VM, ANY, ANY, VM, VM],
        scratch_shapes=[
            pltpu.VMEM((count, width), F),
            pltpu.VMEM((count, width), F),
            pltpu.VMEM((count, hidden), BF),
            pltpu.VMEM((count, hidden), BF),
            pltpu.VMEM(wp.shape, BF),
            pltpu.VMEM(wd.shape, BF),
            pltpu.VMEM(wg.shape, BF),
            pltpu.VMEM(wu.shape, BF),
            pltpu.VMEM((count, hidden), BF),
            pltpu.VMEM((count, hidden), BF),
            pltpu.VMEM((count, width), F),
            pltpu.VMEM((count, width), F),
            pltpu.SemaphoreType.DMA((8,)),
            pltpu.SemaphoreType.DMA((2,)),
        ],
        compiler_params=pltpu.CompilerParams(vmem_limit_bytes=VMEM_LIMIT),
        cost_estimate=cost(4e9, 30e6),
        name="query_back",
    )(d_emb, saved["proj"], gains, saved["h2"], saved["hid"], saved["gv"], saved["us"], wp, wd, wg, wu, after)


def split_out(own, grads, keep_h, send_h, sem):
    first = pltpu.make_async_copy(grads.at[own], keep_h, sem.at[0])
    second = pltpu.make_async_copy(grads.at[1 - own], send_h, sem.at[1])
    first.start()
    second.start()
    return first, second


def doc_top_kernel(
    n_arrays, own, number, d_emb_in, demb, mask, rep, coef, proj, gains, wp, d_proj_q, d_ffn_q,
    h2_h, act_h, act_qh, n3_h, n3_qh,
    *refs,
):
    every = refs[:n_arrays]
    (
    d_h2, d_ffn, g_gain, keep_h, send_h,
    h2, act, n3, d_proj, d_all, acc, grads, sem_in, sem_out,
    ) = refs[n_arrays:]
    count = demb.shape[0]
    rest = d_ffn_q.shape[0]
    loads = [
        pltpu.make_async_copy(src, dst, sem_in.at[i])
        for i, (src, dst) in enumerate(
            (
                (h2_h, h2),
                (act_h, act.at[0:count]),
                (act_qh, act.at[count:]),
                (n3_h, n3.at[0:count]),
                (n3_qh, n3.at[count:]),
            )
        )
    ]
    for copy in loads:
        copy.start()
    acc[...] = d_emb_in[...].astype(F)
    per = mask.shape[2] * QUERY_LENGTH // 256

    def sims(slot, qb):
        row = number[slot]
        e = jnp.exp(mm_nt(demb[...], qb) * SCALE)
        m = mm(mask[row // per], rep[:, pl.ds(pl.multiple_of((row % per) * 256, 256), 256)])
        ds = (e * m * coef[pl.ds(row, 1), :]).astype(BF)
        acc[...] += mm(ds, qb)

    each_block(every, 256, sims)
    loads[0].wait()
    dp, dh, gg = top_rows(acc[...], proj[...], h2[...], gains[2:3, :], wp[...])
    d_proj[0:count, :] = dp
    d_proj[count:, :] = d_proj_q[...]
    d_h2[...] = dh
    g_gain[...] = jnp.zeros_like(g_gain)
    g_gain[0:1, :] = gg
    d_ffn[...] = dh.astype(BF)
    d_all[0:count, :] = dh.astype(BF)
    d_all[count:, :] = d_ffn_q[...]
    for copy in loads[1:]:
        copy.wait()
    gp = mm_tn(n3[...], d_proj[...])
    grads[:, :, :, :, 192:224, :] = jnp.zeros((2, 4, 2, 2, 32, 256), BF)
    for w in range(8):
        for r in range(3):
            lo = 96 * w + 32 * r
            grads[w % 2, w // 2, r // 2, r % 2, 192:224, 0:128] = gp[lo : lo + 32, :].astype(BF)

    def down(w, carry):
        g = mm_tn(act[:, pl.ds(pl.multiple_of(w * 256, 256), 256)], d_all[...])
        for r in range(4):
            for c in range(3):
                grads[w % 2, w // 2, r // 2, r % 2, 64 * c : 64 * c + 64, :] = g[
                    64 * r : 64 * r + 64, 256 * c : 256 * c + 256
                ].astype(BF)
        return carry

    lax.fori_loop(0, 8, down, 0)
    for copy in split_out(own[0], grads, keep_h, send_h, sem_out):
        copy.wait()


def doc_top(own, number, d_emb, demb, every, mask, rep, coef, dsaved, qsaved, gains, wp, d_proj_q, d_ffn_q):
    count, width = dsaved["h2"].shape
    rest = d_ffn_q.shape[0]
    hidden = dsaved["act"].shape[1]
    emb = wp.shape[1]
    piece = sds((4, 2, 2, 224, 256), BF)
    return pl.pallas_call(
        functools.partial(doc_top_kernel, len(every)),
        out_shape=(sds((count, width), F), sds((count, width), BF), sds((8, width), F), piece, piece),
        in_specs=[SM] * 2 + [VM] * 10 + [ANY] * 5 + [VM] * len(every),
        out_specs=[VM] * 3 + [ANY] * 2,
        scratch_shapes=[
            pltpu.VMEM((count, width), F),
            pltpu.VMEM((count + rest, hidden), BF),
            pltpu.VMEM((count + rest, width), BF),
            pltpu.VMEM((count + rest, emb), BF),
            pltpu.VMEM((count + rest, width), BF),
            pltpu.VMEM((count, emb), F),
            pltpu.VMEM((2, 4, 2, 2, 224, 256), BF),
            pltpu.SemaphoreType.DMA((5,)),
            pltpu.SemaphoreType.DMA((2,)),
        ],
        compiler_params=pltpu.CompilerParams(vmem_limit_bytes=VMEM_LIMIT),
        cost_estimate=cost(6e9, 10e6),
        name="doc_top",
    )(
        own, number, d_emb, demb, mask, rep, coef, dsaved["proj"], gains, wp, d_proj_q, d_ffn_q,
        dsaved["h2"], dsaved["act"], qsaved["act"], dsaved["n3"], qsaved["n3"], *every,
    )


def ffn_grads_kernel(
    own, d_ffn, n2_d, n2_q, wd_h, us_h, gv_h, gate_qh, up_qh,
    gate_h, up_h, keep_h, send_h,
    wd, us, gv, gate, up, n2t, grads, sem_in, sem_out,
):
    count = d_ffn.shape[0]
    loads = [
        pltpu.make_async_copy(src, dst, sem_in.at[i])
        for i, (src, dst) in enumerate(
            (
                (wd_h, wd),
                (us_h, us),
                (gv_h, gv),
                (gate_qh, gate.at[count:]),
                (up_qh, up.at[count:]),
            )
        )
    ]
    for copy in loads:
        copy.start()
    n2t[:, 0:count] = jnp.transpose(n2_d[...])
    n2t[:, count:] = jnp.transpose(n2_q[...])
    for copy in loads:
        copy.wait()

    def tile(t, carry):
        cols = pl.ds(pl.multiple_of(t * 512, 512), 512)
        d_act = mm_nt(d_ffn[...], wd[cols, :])
        gate[0:count, cols] = (d_act * us[:, cols].astype(F)).astype(BF)
        up[0:count, cols] = (d_act * gv[:, cols].astype(F)).astype(BF)
        for base, source in ((0, gate), (1, up)):
            g = mm(n2t[...], source[:, cols]).astype(BF)
            for c in range(2):
                start = pl.multiple_of((t % 2) * 192 + 96 * c, 96)
                for w in range(8):
                    grads[w % 2, w // 2, base, t // 2, pl.ds(start, 96), :] = g[
                        96 * w : 96 * w + 96, 256 * c : 256 * c + 256
                    ]
        return carry

    lax.fori_loop(0, wd.shape[0] // 512, tile, 0)
    copies = [
        pltpu.make_async_copy(gate.at[0:count], gate_h, sem_out.at[2]),
        pltpu.make_async_copy(up.at[0:count], up_h, sem_out.at[3]),
    ]
    for copy in copies:
        copy.start()
    for copy in tuple(split_out(own[0], grads, keep_h, send_h, sem_out)) + tuple(copies):
        copy.wait()


def ffn_grads(own, d_ffn, dsaved, qsaved, wd, gate_q, up_q):
    count, width = d_ffn.shape
    rest, hidden = gate_q.shape
    piece = sds((4, 2, 2, 384, 256), BF)
    return pl.pallas_call(
        ffn_grads_kernel,
        out_shape=(sds((count, hidden), BF), sds((count, hidden), BF), piece, piece),
        in_specs=[SM] + [VM] * 3 + [ANY] * 5,
        out_specs=[ANY] * 4,
        scratch_shapes=[
            pltpu.VMEM(wd.shape, BF),
            pltpu.VMEM((count, hidden), BF),
            pltpu.VMEM((count, hidden), BF),
            pltpu.VMEM((count + rest, hidden), BF),
            pltpu.VMEM((count + rest, hidden), BF),
            pltpu.VMEM((width, count + rest), BF),
            pltpu.VMEM((2, 4, 2, 2, 384, 256), BF),
            pltpu.SemaphoreType.DMA((5,)),
            pltpu.SemaphoreType.DMA((4,)),
        ],
        compiler_params=pltpu.CompilerParams(vmem_limit_bytes=VMEM_LIMIT),
        cost_estimate=cost(8e9, 20e6),
        name="ffn_grads",
    )(own, d_ffn, dsaved["n2"], qsaved["n2"], wd, dsaved["us"], dsaved["gv"], gate_q, up_q)


def middle_back_kernel(
    d_h2, hid, d_hid_q, gains,
    wg_h, wu_h, wo_h, gate_h, up_h, li_d, li_q, *refs
):
    d_hid, g_gain, d_attn, g, wg, wu, wo, gate, up, li, sem_in = refs[-11:]
    count = d_h2.shape[0]
    rest = d_hid_q.shape[0]
    loads = [
        pltpu.make_async_copy(src, dst, sem_in.at[i])
        for i, (src, dst) in enumerate(
            (
                (wg_h, wg),
                (gate_h, gate),
                (wu_h, wu),
                (up_h, up),
                (wo_h, wo),
                (li_d, li.at[0:count]),
                (li_q, li.at[count:]),
            )
        )
    ]
    for copy in loads:
        copy.start()
    for copy in loads[0:4]:
        copy.wait()
    gain_f = gains[1:2, :]
    g_gain[...] = jnp.zeros_like(g_gain)

    def through(rows):
        d_n2 = mm_nt(gate[rows, :], wg[...]) + mm_nt(up[rows, :], wu[...])
        dm, gg = rms_back(hid[rows, :], gain_f, d_n2)
        total = d_h2[rows, :] + dm
        d_hid[rows, :] = total
        g_gain[0:1, :] += gg
        d_attn[rows, :] = total.astype(BF)

    rows_loop(count, 256, through)
    d_attn[count:, :] = d_hid_q[...].astype(BF)
    for copy in loads[4:]:
        copy.wait()

    def to_context(rows):
        d_context = mm_nt(d_attn[rows, :], wo[...]).astype(BF).astype(F)
        g[rows, :] = (d_context * li[rows, :]).astype(BF)

    rows_loop(count + rest, 256, to_context)


def middle_back(d_h2, d_hid_q, gate, up, dsaved, qsaved, weights, gains, after):
    wq, wk, wv, wo, wg, wu, wd, wp = weights
    count, width = d_h2.shape
    rows = count + d_hid_q.shape[0]
    hidden = wg.shape[1]
    return pl.pallas_call(
        middle_back_kernel,
        out_shape=(sds((count, width), F), sds((8, width), F), sds((rows, width), BF), sds((rows, width), BF)),
        in_specs=[VM] * 4 + [ANY] * (7 + len(after)),
        out_specs=[VM] * 4,
        scratch_shapes=[
            pltpu.VMEM(wg.shape, BF),
            pltpu.VMEM(wu.shape, BF),
            pltpu.VMEM(wo.shape, BF),
            pltpu.VMEM((count, hidden), BF),
            pltpu.VMEM((count, hidden), BF),
            pltpu.VMEM((rows, width), F),
            pltpu.SemaphoreType.DMA((7,)),
        ],
        compiler_params=pltpu.CompilerParams(vmem_limit_bytes=VMEM_LIMIT),
        cost_estimate=cost(5e9, 20e6),
        name="middle_back",
    )(d_h2, dsaved["hid"], d_hid_q, gains, wg, wu, wo, gate, up, dsaved["li"], qsaved["li"], *after)


def attn_back_kernel(
    own, hot, d_attn, g,
    n1_d, n1_q, q_d, q_q, k_d, k_q, v_d, v_q, li_d, li_q, ctx_d, ctx_q, p_dh, p_qh, *refs
):
    (
    dq_h, dk_h, dv_h, g_rel, keep_h, send_h,
    n1, q, k, v, li, ctx, p_d, p_q,
    dq, dk, dv, ds, acc, sums, n1t, grads, sem_in, sem_out,
    ) = refs[-24:]
    count = q_d.shape[0]
    rest = q_q.shape[0]
    heads = p_d.shape[0]
    loads = [
        pltpu.make_async_copy(src, dst, sem_in.at[i])
        for i, (src, dst) in enumerate(
            (
                (li_d, li.at[0:count]),
                (li_q, li.at[count:]),
                (q_d, q.at[0:count]),
                (q_q, q.at[count:]),
                (k_d, k.at[0:count]),
                (k_q, k.at[count:]),
                (v_d, v.at[0:count]),
                (v_q, v.at[count:]),
                (p_dh, p_d),
                (p_qh, p_q),
                (ctx_d, ctx.at[0:count]),
                (ctx_q, ctx.at[count:]),
                (n1_d, n1.at[0:count]),
                (n1_q, n1.at[count:]),
            )
        )
    ]
    for copy in loads:
        copy.start()

    def put(which, value):
        value = value.astype(BF)
        for w in range(8):
            for c in range(3):
                grads[w % 2, w // 2, which // 2, which % 2, 96 * c : 96 * c + 96, :] = value[
                    96 * w : 96 * w + 96, 256 * c : 256 * c + 256
                ]

    for copy in loads[0:10]:
        copy.wait()
    sums[...] = jnp.zeros_like(sums)
    low, high, _, _ = half_masks()

    def pair(index, carry):
        lanes = pl.ds(pl.multiple_of(index * 128, 128), 128)
        q2 = q[:, lanes]
        k2 = k[:, lanes]
        v2 = v[:, lanes]
        g2 = g[:, lanes]
        l2 = li[:, lanes]
        d_q = jnp.zeros((count, 128), F)
        d_k = jnp.zeros((count, 128), F)
        d_v = jnp.zeros((count, 128), F)
        d_qq = [jnp.zeros((128, 128), F)] * (rest // 128)
        d_kq = [jnp.zeros((128, 128), F)] * (rest // 128)
        d_vq = [jnp.zeros((128, 128), F)] * (rest // 128)
        for e, keep in enumerate((low, high)):
            head = 2 * index + e
            keep = keep.astype(BF)
            km = k2 * keep
            vm = v2 * keep
            qm = q2 * keep
            gm = g2 * keep
            share = l2[:, 64 * e : 64 * e + 1]
            acc[...] = jnp.zeros_like(acc)
            for i in range(count // 128):
                rows = slice(128 * i, 128 * i + 128)
                d_p = mm_nt(g2[rows], vm[0:count])
                pf = p_d[head, rows, :].astype(F)
                t = pf * d_p
                dsb = (t - pf * (share[rows] * jnp.sum(t, axis=1, keepdims=True))).astype(BF)
                ds[rows, :] = dsb
                acc[:, SHIFT - 128 * i : SHIFT - 128 * i + DL] += dsb.astype(F)
            d_q = d_q + mm(ds[...], km[0:count])
            d_k = d_k + mm_tn(ds[...], qm[0:count])
            d_v = d_v + mm_tn(p_d[head], gm[0:count])
            for i in range(rest // 128):
                rows = slice(count + 128 * i, count + 128 * i + 128)
                d_p = mm_nt(g2[rows], vm[rows])
                pb = p_q[head, 128 * i : 128 * i + 128, :]
                pf = pb.astype(F)
                t = pf * d_p
                dsb = (t - pf * (share[rows] * jnp.sum(t, axis=1, keepdims=True))).astype(BF)
                acc[:, SHIFT : SHIFT + 128] += dsb.astype(F)
                d_qq[i] = d_qq[i] + mm(dsb, km[rows])
                d_kq[i] = d_kq[i] + mm_tn(dsb, qm[rows])
                d_vq[i] = d_vq[i] + mm_tn(pb, gm[rows])
            folded = acc[...]
            half = 64
            while half >= 8:
                folded = folded[0:half] + pltpu.roll(folded[half : 2 * half], TABLE - half, 1)
                half //= 2
            line = folded[0:1]
            for i in range(1, 8):
                line = line + pltpu.roll(folded[i : i + 1], TABLE - i, 1)
            sums[pl.ds(head, 1), :] = line
        dq[0:count, lanes] = d_q.astype(BF)
        dk[0:count, lanes] = d_k.astype(BF)
        dv[0:count, lanes] = d_v.astype(BF)
        for i in range(rest // 128):
            rows = slice(count + 128 * i, count + 128 * i + 128)
            dq[rows, lanes] = d_qq[i].astype(BF)
            dk[rows, lanes] = d_kq[i].astype(BF)
            dv[rows, lanes] = d_vq[i].astype(BF)
        return carry

    lax.fori_loop(0, heads // 2, pair, 0)
    copies = [
        pltpu.make_async_copy(src, dst, sem_out.at[2 + i])
        for i, (src, dst) in enumerate(((dq, dq_h), (dk, dk_h), (dv, dv_h)))
    ]
    for copy in copies:
        copy.start()
    for copy in loads[10:]:
        copy.wait()
    n1t[...] = jnp.transpose(n1[...])
    put(0, mm(n1t[...], dq[...]))
    put(1, mm(n1t[...], dk[...]))
    put(2, mm(n1t[...], dv[...]))
    put(3, mm_tn(ctx[...], d_attn[...]))
    out = split_out(own[0], grads, keep_h, send_h, sem_out)
    g_rel[...] = lax.dot_general(
        sums[...], hot[...], (((1,), (1,)), ((), ())),
        preferred_element_type=F, precision=lax.Precision.HIGHEST,
    )
    for copy in tuple(out) + tuple(copies):
        copy.wait()


def attn_back(own, d_attn, g, dsaved, qsaved, hot, after):
    rows, width = d_attn.shape
    heads = dsaved["p"].shape[0]
    buckets = hot.shape[0]
    piece = sds((4, 2, 2, 288, 256), BF)
    full = sds((rows, width), BF)
    both = []
    for name in ("n1", "q", "k", "v", "li", "ctx", "p"):
        both += [dsaved[name], qsaved[name]]
    return pl.pallas_call(
        attn_back_kernel,
        out_shape=(full, full, full, sds((16, buckets), F), piece, piece),
        in_specs=[SM] + [VM] * 3 + [ANY] * (14 + len(after)),
        out_specs=[ANY] * 3 + [VM] + [ANY] * 2,
        scratch_shapes=[pltpu.VMEM((rows, width), BF)] * 4
        + [
            pltpu.VMEM((rows, width), F),
            pltpu.VMEM((rows, width), BF),
            pltpu.VMEM(dsaved["p"].shape, BF),
            pltpu.VMEM(qsaved["p"].shape, BF),
            pltpu.VMEM((rows, width), BF),
            pltpu.VMEM((rows, width), BF),
            pltpu.VMEM((rows, width), BF),
            pltpu.VMEM((DL, DL), BF),
            pltpu.VMEM((128, TABLE), F),
            pltpu.VMEM((16, TABLE), F),
            pltpu.VMEM((width, rows), BF),
            pltpu.VMEM((2, 4, 2, 2, 288, 256), BF),
            pltpu.SemaphoreType.DMA((14,)),
            pltpu.SemaphoreType.DMA((5,)),
        ],
        compiler_params=pltpu.CompilerParams(vmem_limit_bytes=VMEM_LIMIT),
        cost_estimate=cost(15e9, 40e6),
        name="attn_back",
    )(own, hot, d_attn, g, *both, *after)


def input_back_kernel(
    tok_d, tok_q, d_hid_d, d_hid_q, gains, dq, dk, dv, wq, wk, wv, gain_f, gain_l, gains_q, g_rel,
    parts, *refs
):
    out_d, out_q, small, g_gain = refs[-4:]
    count = tok_d.shape[0]
    gain_a = gains[0:1, :]
    g_gain[...] = jnp.zeros_like(g_gain)

    def part(offset, tok, d_hid, out):
        def step(rows):
            at = pl.ds(pl.multiple_of(rows.start + offset, 256), 256)
            d_n1 = mm_nt(dq[at, :], wq[...]) + mm_nt(dk[at, :], wk[...]) + mm_nt(dv[at, :], wv[...])
            d_in, gg = rms_back(tok[rows, :].astype(F), gain_a, d_n1)
            g_gain[0:1, :] += gg
            out[rows, :] = (d_hid[rows, :] + d_in).astype(BF)

        rows_loop(tok.shape[0], 256, step)

    part(0, tok_d, d_hid_d, out_d)
    part(count, tok_q, d_hid_q, out_q)
    small[...] = jnp.zeros_like(small)
    rows = (
        g_gain[0:1, :],
        gain_f[0:1, :] + gains_q[0:1, :],
        gain_l[0:1, :] + gains_q[1:2, :],
    )
    for i, row in enumerate(rows):
        for c in range(6):
            small[8 * i + c : 8 * i + c + 1, :] = row[:, 128 * c : 128 * c + 128]
    small[24:25, :] = parts[0:1, :]
    small[32:48, 0 : g_rel.shape[1]] = g_rel[...]


def input_back(tok_d, tok_q, d_hid_d, d_hid_q, gains, dq, dk, dv, weights, extra, after):
    width = tok_d.shape[1]
    return pl.pallas_call(
        input_back_kernel,
        out_shape=(sds(tok_d.shape, BF), sds(tok_q.shape, BF), sds((48, 128), F)),
        in_specs=[VM] * 16 + [ANY] * len(after),
        out_specs=[VM] * 3,
        scratch_shapes=[pltpu.VMEM((8, width), F)],
        compiler_params=pltpu.CompilerParams(vmem_limit_bytes=VMEM_LIMIT),
        cost_estimate=cost(3e9, 10e6),
        name="input_back",
    )(tok_d, tok_q, d_hid_d, d_hid_q, gains, dq, dk, dv, weights[0], weights[1], weights[2], *extra, *after)


def unpack_kernel(which, me, a_own, a_came, b_own, b_came, *refs):
    stack = refs[-1]
    outs = refs[-1 - (4 if which == "attn" else 2) : -1]
    half = a_own.shape[1]
    y, x = me[0], me[1]
    for i in range(2):
        stack[i, x, 0:half, :] = a_own[i]
        stack[i, 1 - x, 0:half, :] = a_came[i]
        stack[y, i, half:, :] = b_own[i]
        stack[1 - y, i, half:, :] = b_came[i]
    if which == "ffn":
        for r in range(4):
            out = outs[r // 2]
            for c in range(4):
                at = (r % 2) * 1024 + 256 * c
                out[:, at : at + 256] = stack[r // 2, r % 2, 96 * c : 96 * c + 96, :].astype(F)
    elif which == "attn":
        for r in range(4):
            for c in range(3):
                outs[r][:, 256 * c : 256 * c + 256] = stack[
                    r // 2, r % 2, 96 * c : 96 * c + 96, :
                ].astype(F)
    else:
        for r in range(4):
            for c in range(3):
                outs[0][64 * r : 64 * r + 64, 256 * c : 256 * c + 256] = stack[
                    r // 2, r % 2, 64 * c : 64 * c + 64, :
                ].astype(F)
        for r in range(3):
            outs[1][32 * r : 32 * r + 32, :] = stack[r // 2, r % 2, 192:224, 0:128].astype(F)


def unpack(which, me, parts, shapes, after):
    half = parts[0].shape[1]
    return pl.pallas_call(
        functools.partial(unpack_kernel, which),
        out_shape=tuple(sds(s, F) for s in shapes),
        in_specs=[SM] + [VM] * 4 + [ANY] * len(after),
        out_specs=tuple(VM for _ in shapes),
        scratch_shapes=[pltpu.VMEM((2, 2, 2 * half, 256), BF)],
        compiler_params=pltpu.CompilerParams(vmem_limit_bytes=VMEM_LIMIT),
        cost_estimate=cost(1e6, 3e6),
        name="unpack_" + which,
    )(me, *parts, *after)


def swap(values, axis, size, mask):
    return lax.ppermute(values, axis, [(i, i ^ mask) for i in range(size)])


def near_kernel(me, keep, came, *refs):
    send_a, send_b, own_a, own_b = refs[-4:]
    y, x = me[0], me[1]
    half = own_a.shape[2]

    def total(i, k, low):
        part = keep[0, i, k, low : low + half, :].astype(F) + came[0, i, k, low : low + half, :].astype(F)
        return part.astype(BF)

    for i in range(2):
        send_a[0, i] = total(i, 1 - x, 0)
        own_a[0, i] = total(i, x, 0)
        send_b[0, i] = total(1 - y, i, half)
        own_b[0, i] = total(y, i, half)


def line_kernel(me, a, came_a, b, came_b, *refs):
    z = me[2]
    for m, out in enumerate(refs[-4:]):
        out[0] = (a[z ^ m].astype(F) + came_a[z ^ m].astype(F)).astype(BF)
        out[1] = (b[z ^ m].astype(F) + came_b[z ^ m].astype(F)).astype(BF)


def far_kernel(own, one, two, three, *refs):
    for i, out in enumerate(refs[-2:]):
        total = own[i].astype(F) + one[i].astype(F) + two[i].astype(F) + three[i].astype(F)
        out[...] = total.astype(BF)


def back_kernel(a, came_a, b, came_b, *refs):
    out_a, out_b = refs[-2:]
    out_a[...] = (a[...].astype(F) + came_a[...].astype(F)).astype(BF)
    out_b[...] = (b[...].astype(F) + came_b[...].astype(F)).astype(BF)


def sum_two_kernel(a, b, *refs):
    refs[-1][...] = a[...] + b[...]


def sum_two(a, b, after):
    return pl.pallas_call(
        sum_two_kernel,
        out_shape=sds(a.shape, F),
        in_specs=[VM] * 2 + [ANY] * len(after),
        out_specs=VM,
        cost_estimate=cost(1e4, 1e5),
        name="sum_two",
    )(a, b, *after)


def sum_four_kernel(which, me, own, one, two, three, *refs):
    out, stack = refs[-2:]
    for m, part in enumerate((own, one, two, three)):
        stack[me[which] ^ m] = part[...]
    out[...] = stack[0] + stack[1] + stack[2] + stack[3]


def sum_four(me, which, own, came, after):
    return pl.pallas_call(
        functools.partial(sum_four_kernel, which),
        out_shape=sds(own.shape, F),
        in_specs=[SM] + [VM] * 4 + [ANY] * len(after),
        out_specs=VM,
        scratch_shapes=[pltpu.VMEM((4,) + own.shape, F)],
        cost_estimate=cost(1e4, 1e5),
        name="sum_four",
    )(me, own, *came, *after)


class Reduction:
    def __init__(self, name, me, keep, send):
        self.name = name
        self.me = me
        self.half = keep.shape[3] // 2
        self.keep = keep
        self.came = swap(send, "wide", 8, 1)

    def near(self, after):
        rows = 2 * self.half
        whole = pl.BlockSpec((1, 2, 2, rows, 256), lambda i: (i, 0, 0, 0, 0))
        part = pl.BlockSpec((1, 2, self.half, 256), lambda i: (i, 0, 0, 0))
        send_a, send_b, self.a, self.b = pl.pallas_call(
            near_kernel,
            grid=(4,),
            out_shape=(sds((4, 2, self.half, 256), BF),) * 4,
            in_specs=[SM, whole, whole] + [ANY] * len(after),
            out_specs=(part,) * 4,
            compiler_params=pltpu.CompilerParams(vmem_limit_bytes=VMEM_LIMIT),
            cost_estimate=cost(1e6, rows * 256 * 2 * 48),
            name="near_" + self.name,
        )(self.me, self.keep, self.came, *after)
        self.came_a = swap(send_a, "rep", 4, 1)
        self.came_b = swap(send_b, "rep", 4, 2)
        return (self.a,)

    def line(self, after):
        outs = pl.pallas_call(
            line_kernel,
            out_shape=(sds((2, 2, self.half, 256), BF),) * 4,
            in_specs=[SM] + [VM] * 4 + [ANY] * len(after),
            out_specs=(VM,) * 4,
            compiler_params=pltpu.CompilerParams(vmem_limit_bytes=VMEM_LIMIT),
            cost_estimate=cost(1e6, self.half * 256 * 2 * 48),
            name="line_" + self.name,
        )(self.me, self.a, self.came_a, self.b, self.came_b, *after)
        self.own = outs[0]
        self.came = [swap(outs[m], "wide", 8, 2 * m) for m in (1, 2, 3)]
        return (self.own,)

    def far(self, after):
        self.a, self.b = pl.pallas_call(
            far_kernel,
            out_shape=(sds((2, self.half, 256), BF),) * 2,
            in_specs=[VM] * 4 + [ANY] * len(after),
            out_specs=(VM,) * 2,
            compiler_params=pltpu.CompilerParams(vmem_limit_bytes=VMEM_LIMIT),
            cost_estimate=cost(1e6, self.half * 256 * 2 * 20),
            name="far_" + self.name,
        )(self.own, *self.came, *after)
        self.came_a = swap(self.a, "rep", 4, 2)
        self.came_b = swap(self.b, "rep", 4, 1)
        return (self.a,)

    def back(self, after):
        self.a, self.b = pl.pallas_call(
            back_kernel,
            out_shape=(sds((2, self.half, 256), BF),) * 2,
            in_specs=[VM] * 4 + [ANY] * len(after),
            out_specs=(VM,) * 2,
            compiler_params=pltpu.CompilerParams(vmem_limit_bytes=VMEM_LIMIT),
            cost_estimate=cost(1e6, self.half * 256 * 2 * 12),
            name="back_" + self.name,
        )(self.a, self.came_a, self.b, self.came_b, *after)
        self.came_a = swap(self.a, "rep", 4, 1)
        self.came_b = swap(self.b, "rep", 4, 2)
        return (self.a,)

    def unpack(self, shapes, after):
        return unpack(self.name, self.me, (self.a, self.came_a, self.b, self.came_b), shapes, after)


def natural(which, keep, send):
    both = jnp.stack([keep, send])
    both = both.reshape((2, 4, 4) + both.shape[4:])
    if which == "ffn":
        a = both.reshape(2, 4, 4, 4, 96, 256).transpose(1, 0, 4, 2, 3, 5).reshape(768, 4096)
        return [a[:, :2048], a[:, 2048:]]
    if which == "attn":
        a = both.reshape(2, 4, 4, 3, 96, 256).transpose(2, 1, 0, 4, 3, 5).reshape(4, 768, 768)
        return [a[i] for i in range(4)]
    d = both[:, :, :, :192].reshape(2, 4, 4, 3, 64, 256).transpose(1, 0, 2, 4, 3, 5)
    e = both[:, :, :3, 192:224, :128].transpose(1, 0, 2, 3, 4)
    return [d.reshape(2048, 768), e.reshape(768, 128)]


def body(
    doc_tokens, query_tokens, doc_cotangent, query_cotangent, retrieved, pos_ids, pos_count,
    w_query, w_key, carried_content_weights, w_out, w_gate, w_up, w_down, w_proj,
    gain_attn, gain_ffn, gain_final, rel_bias,
):
    n_wide = lax.axis_size("wide")
    n_rep = lax.axis_size("rep")
    fast = n_wide == 8 and n_rep == 4
    weights = (w_query, w_key, carried_content_weights, w_out, w_gate, w_up, w_down, w_proj)
    width = doc_tokens.shape[1]
    gains = jnp.stack([gain_attn, gain_ffn, gain_final]).astype(F)
    buckets, heads = rel_bias.shape
    hot_np = bucket_hot(buckets)
    hot = jnp.asarray(hot_np, BF)
    hot_f = jnp.asarray(hot_np, F)
    rel = jnp.transpose(rel_bias)
    group = retrieved.shape[1]
    queries = pos_ids.shape[0]
    wide = lax.axis_index("wide").astype(jnp.int32)
    z, core = wide // 2, wide % 2

    mask_rows = jnp.transpose(retrieved).astype(F)
    mask_query = lax.all_to_all(mask_rows, "wide", 0, 0, tiled=True).reshape(n_wide, queries, DL)
    blocks = group // 64
    mask_doc = retrieved.astype(BF).reshape(DL, blocks, 64).transpose(1, 0, 2)
    rep_hot = jnp.asarray(query_hot(64), BF)

    def line_swaps(emb):
        return [emb] + [swap(emb, "wide", n_wide, 2 * m) for m in (1, 2, 3)]

    doc = layer_forward(doc_tokens, weights, gains, rel, hot, DL)
    if fast:
        number = jnp.stack(
            [(z ^ m) * 2 + core for m in range(4)] + [(z ^ m) * 2 + 1 - core for m in range(4)]
        )
        docs = line_swaps(doc["emb"])
    else:
        number = jnp.arange(n_wide, dtype=jnp.int32)
        docs = [lax.all_gather(doc["emb"], "wide", axis=0, tiled=True)]
    query = layer_forward(
        query_tokens, weights, gains, rel, hot, QUERY_LENGTH, (doc["emb"], mask_query)
    )
    if fast:
        docs = docs + [swap(d, "wide", n_wide, 1) for d in docs]
        every = line_swaps(query["emb"])
    else:
        every = [lax.all_gather(query["emb"], "wide", axis=0, tiled=True)]

    coef, d_query_emb, parts = query_sims(
        number, query["emb"], docs, mask_query, pos_ids, pos_count.reshape(queries, 1), query_cotangent
    )
    coef_all = lax.all_to_all(coef, "wide", 0, 0, tiled=True)
    if fast:
        every = every + [swap(e, "wide", n_wide, 1) for e in every]
    own = (core if fast else jnp.int32(0)).reshape(1)
    d_proj_q, d_ffn_q, d_gate_q, d_up_q, d_hid_q, gains_q = query_back(
        d_query_emb, query, weights, gains, coef
    )
    d_h2, d_ffn, gain_l, keep_down, send_down = doc_top(
        own, number, doc_cotangent, doc["emb"], every, mask_doc, rep_hot, coef_all, doc, query, gains,
        w_proj, d_proj_q, d_ffn_q,
    )
    d_gate, d_up, keep_ffn, send_ffn = ffn_grads(own, d_ffn, doc, query, w_down, d_gate_q, d_up_q)
    after = ()
    if fast:
        rep = lax.axis_index("rep").astype(jnp.int32)
        me = jnp.stack([rep // 2, rep % 2, z, rep])
        down = Reduction("down", me, keep_down, send_down)
        ffn = Reduction("ffn", me, keep_ffn, send_ffn)
        after = down.near((d_up,))
    d_hid, gain_f, d_attn, g = middle_back(
        d_h2, d_hid_q, d_gate, d_up, doc, query, weights, gains, after
    )
    if fast:
        after = ffn.near((d_attn,))
        after = down.line(after)
    dq, dk, dv, g_rel, keep_attn, send_attn = attn_back(own, d_attn, g, doc, query, hot_f, after)
    if fast:
        attn = Reduction("attn", me, keep_attn, send_attn)
        after = down.far((g_rel,))
        after = ffn.line(after)
    doc_grad, query_grad, small = input_back(
        doc_tokens, query_tokens, d_hid, d_hid_q, gains, dq, dk, dv, weights,
        (gain_f, gain_l, gains_q, g_rel, parts), after,
    )
    if fast:
        after = attn.near((small,))
        small = sum_two(small, swap(small, "wide", 8, 1), after)
        after = down.back((small,))
        came = [swap(small, "rep", 4, m) for m in (1, 2, 3)]
        after = ffn.far(after)
        small = sum_four(me, 3, small, came, after)
        came = [swap(small, "wide", 8, 2 * m) for m in (1, 2, 3)]
        after = attn.line((small,))
        after = grad_down, grad_proj = down.unpack(((256, 768), (96, 128)), after)
        small = sum_four(me, 2, small, came, after[1:])
        after = ffn.back((small,))
        after = attn.far(after)
        after = grad_gate, grad_up = ffn.unpack(((96, 2048), (96, 2048)), after)
        after = attn.back(after[1:])
        grad_query, grad_key, grad_value, grad_out = attn.unpack(((96, 768),) * 4, after)
    else:
        small = lax.psum(small, ("rep", "wide"))
        shards = []
        for which, keep, send in (
            ("attn", keep_attn, send_attn),
            ("ffn", keep_ffn, send_ffn),
            ("down", keep_down, send_down),
        ):
            for whole in natural(which, keep, send):
                part = lax.psum_scatter(whole, "wide", scatter_dimension=0, tiled=True)
                shards.append(lax.psum(part, "rep").astype(F))
        (
            grad_query, grad_key, grad_value, grad_out, grad_gate, grad_up, grad_down, grad_proj,
        ) = shards
    loss = small[24, 0] / (queries * n_wide * n_rep)
    fraction = small[24, 1] / (DL * small[24, 2])
    return (
        doc["emb"],
        query["emb"],
        doc_grad,
        query_grad,
        grad_query,
        grad_key,
        grad_value,
        grad_out,
        grad_gate,
        grad_up,
        grad_down,
        grad_proj,
        small[0:6].reshape(width),
        small[8:14].reshape(width),
        small[16:22].reshape(width),
        jnp.transpose(small[32 : 32 + heads, 0:buckets]),
        loss,
        fraction,
    )


def solution(mesh):
    rows = P(("rep", "wide"), None)
    return jax.shard_map(
        body,
        mesh=mesh,
        in_specs=(rows,) * 6 + (P(("rep", "wide")),) + (P(),) * 12,
        out_specs=(rows,) * 4 + (P("wide", None),) * 8 + (P(),) * 6,
        check_vma=False,
    )
```

time: 803 us -> 337 us (0.42)
  waiting for transfers between devices: 265 us -> 41.2 us
  matrix products: 197 us -> 0 us
  Pallas kernels: 0 us -> 196 us
  local copies, waits for them, and re-layouts: 138 us -> 16.7 us
  blocking collectives: 72 us -> 0 us
  other arithmetic: 66.6 us -> 2.56 us
  starting transfers between devices: 15.6 us -> 68.2 us
  loops' own time: 21.1 us -> 0 us
  between operations: 20.3 us -> 5.49 us
    reduce_scatter x9 -> x0, waiting for transfers between devices: 231 us -> none  [the longest x1 69.5 us: body(): lax.psum_scatter(grad_down, 'wide', scatter_dimension=0, tiled=True)]
    dot_general x88 -> x0, matrix products: 197 us -> none  [the longest x16 45.9 us: contract_rows(): jnp.einsum('nd,ne->de', left, right, preferred_element_type=jnp.float32)]
    pallas_call x0 -> x27, Pallas kernels: none -> 196 us  [the longest x2 49.5 us: layer_forward(): pl.pallas_call(functools.partial(fwd_kernel, seq, heads, len(after)), out...]
    ppermute x0 -> x51, starting transfers between devices: none -> 58.7 us  [swap(): return lax.ppermute(values, axis, [(i, i ^ mask) for i in range(size)])]
    psum x2 -> x0, blocking collectives: 55.7 us -> none  [the longest x1 38.8 us: body(): lax.psum((doc_attn_small[0] + query_attn_small[0], doc_gains[0] + query_g...]
    convert_element_type x33 -> x1, other arithmetic: 48.3 us -> 0.61 us  [body(): gains = jnp.stack([gain_attn, gain_ffn, gain_final]).astype(F)]
    ppermute x0 -> x51, waiting for transfers between devices: none -> 39.9 us  [swap(): return lax.ppermute(values, axis, [(i, i ^ mask) for i in range(size)])]
    psum x1 -> x0, waiting for transfers between devices: 26.7 us -> none  [body(): lax.psum(shards[0].astype(jnp.bfloat16), 'rep').astype(jnp.float32)]
  transfers between devices with their start and end apart: 13 -> 53, of which waited for: 8 -> 11; matrix products, arithmetic and copies ran while one was open for 38% -> 3% of each run, Pallas kernels for 0% -> 44%
where the time goes in v1:
time: 337 us; the launch traced here: 331 us
  Pallas kernels  196 us (58%)
  starting transfers between devices  68.2 us (20%)
  waiting for transfers between devices  41.2 us (12%)
  local copies, waits for them, and re-layouts  16.7 us (5%)
  between operations  5.49 us (2%)
    ppermute x51, starting transfers between devices, swap(): return lax.ppermute(values, axis, [(i, i ^ mask) for i in range(size)])  58.7 us
    pallas_call x2, Pallas kernels, layer_forward(): pl.pallas_call(functools.partial(fwd_kernel, seq, heads, len(after)), out...  49.5 us
    ppermute x51, waiting for transfers between devices, swap(): return lax.ppermute(values, axis, [(i, i ^ mask) for i in range(size)])  39.9 us
    pallas_call x1, Pallas kernels, attn_back(): pl.pallas_call(attn_back_kernel, out_shape=(full, full, full, sds((16, bu...  33.8 us
    pallas_call x1, Pallas kernels, ffn_grads(): pl.pallas_call(ffn_grads_kernel, out_shape=(sds((count, hidden), BF), sds...  16 us
    pallas_call x1, Pallas kernels, doc_top(): pl.pallas_call(functools.partial(doc_top_kernel, len(every)), out_shape=(...  13.9 us
    pallas_call x3, Pallas kernels, near(): pl.pallas_call(near_kernel, grid=(4,), out_shape=(sds((4, 2, self.half, 2...  13.7 us
    pallas_call x1, Pallas kernels, middle_back(): pl.pallas_call(middle_back_kernel, out_shape=(sds((count, width), F), sds...  13.3 us
  transfers between devices with their start and end apart: 53, of which 11 were waited for; matrix products, arithmetic and copies ran while one was open for 3% of the time, Pallas kernels for 44%

profile of v1, /device:TPU:0, one launch (start us, length us, event | category | flops | bytes accessed | tf_op | source)
XLA Modules:
  0.0 330.8 jit_solution(6191212955065465159)
XLA Ops:
  3.3 31.4 %layer_forward_512.1 = (bf16[512,768]{1,0:T(8,128)(2,1)}, bf16[512,768]{1,0:T(8,128)(2,1)}, bf16[512,768]{1,0:T(8,128)(2,1)}, bf16[512,768]{1,0:T(8,128)(2,1)}, ...) custom-call(bf16[512,768]{1,0:T(8,128)(2,1)} %tok_d.1, ...), custom_call_target="tpu_custom_call" | custom-call | flops 999999995904 | bytes 1 | tf_op jit(solution)/shard_map/layer_forward_512/pallas_call | solution.py:282
  35.3 4.7 %collective-permute-start.2 = (bf16[512,128]{1,0:T(8,128)(2,1)}, bf16[512,128]{1,0:T(8,128)(2,1)}, u32[]{:S(2)}, u32[]{:S(2)}) collective-permute-start(bf16[512,128]{1,0:T(8,128)(2,1)} %get-tuple-element.107.refs_0_.demb), channel_id=1, source_target_pairs={{0,6},{1,7},{2,4},{3,5},{4,2},{5,3},{6,0},{7,1},{8,14},{9,15},{10,... | collective-permute-start | bytes 393224 | tf_op jit(solution)/shard_map/ppermute | solution.py:1014
  41.3 5.6 %all-to-all-start = ((f32[8,8,512]{2,1,0:T(8,128)}), f32[8,8,512]{2,1,0:T(8,128)S(1)}, u32[]{:S(2)}, u32[]{:S(2)}) async-start(f32[8,8,512]{2,1,0:T(8,128)} %convert_bitcast_fusion.1), calls=%async_computation | async-start | bytes 262144 | tf_op jit(solution)/shard_map/all_to_all | solution.py:1194
  55.3 18.1 %layer_forward_32.1 = (bf16[256,768]{1,0:T(8,128)(2,1)}, bf16[256,768]{1,0:T(8,128)(2,1)}, bf16[256,768]{1,0:T(8,128)(2,1)}, bf16[256,768]{1,0:T(8,128)(2,1)}, b...) custom-call(bf16[256,768]{1,0:T(8,128)(2,1)} %tok_q.1, ...), custom_call_target="tpu_custom_call" | custom-call | flops 999999995904 | bytes 1 | tf_op jit(solution)/shard_map/layer_forward_32/pallas_call | solution.py:282
  73.5 2.5 collective-permute-start.9
  78.0 4.1 %query_sims.1 = (f32[8,256]{1,0:T(8,128)}, f32[256,128]{1,0:T(8,128)}, f32[8,128]{1,0:T(8,128)}) custom-call(s32[8]{0:T(128)} %stack.66.number, bf16[256,128]{1,0:T(8,128)(2,1)} %get-tuple-element.108.qemb.refs_0_, f32[8,8,512]{2,1,0:T(8,128)} %copy-done.18, s32[8,4]{1,0:T(8,128)} %copy.44.ids, s32[8,1]{1,0:T(8,128)} %copy.45.used, bf16[256,128]{1,0:T(8,128)(2,1)} %cot.1, ...), custom_call_target="tpu_custom_call" | custom-call | flops 999999995904 | bytes 1 | tf_op jit(solution)/shard_map/query_sims/pallas_call | solution.py:374
  83.4 4.0 %all-to-all-start.1 = ((f32[8,1,256]{2,1,0:T(1,128)}), f32[8,1,256]{2,1,0:T(1,128)}, u32[]{:S(2)}, u32[]{:S(2)}) async-start(f32[8,1,256]{2,1,0:T(1,128)} %copy.46), calls=%async_computation.1 | async-start | bytes 16384 | tf_op jit(solution)/shard_map/all_to_all | solution.py:1223
  88.5 11.9 %query_back.1 = (bf16[256,128]{1,0:T(8,128)(2,1)}, bf16[256,768]{1,0:T(8,128)(2,1)}, bf16[256,2048]{1,0:T(8,128)(2,1)}, bf16[256,2048]{1,0:T(8,128)(2,1)}, f32[256,768]{1,0:T(8,128)}, /*index=5*/f32[8,768]{1,0:T(8,128)}) custom-call(f32[256,128]{1,0:T(8,128)} %get-tuple-element.129.d_emb, f32[256,128]{1,0:T(8,128)} %get-tuple-element.130.proj, ...), custom_call_target="tpu_custom_call" | custom-call | flops 999999995904 | bytes 1 | tf_op jit(solution)/shard_map/query_back/pallas_call | solution.py:454
  101.7 13.9 %doc_top.1 = (f32[512,768]{1,0:T(8,128)}, bf16[512,768]{1,0:T(8,128)(2,1)}, f32[8,768]{1,0:T(8,128)}, bf16[4,2,2,224,256]{4,3,2,1,0:T(8,128)(2,1)}, bf16[4,2,2,224,256]{4,3,2,1,0:T(8,128)(2,1)}) custom-call(s32[1]{0:T(128)} %bitcast.3.own, s32[8]{0:T(128)} %stack.66.number, bf16[512,128]{1,0:T(8,128)(2,1)} %d_emb_in.1, ...), custom_call_target="tpu_custom_call" | custom-call | flops 999999995904 | bytes 1 | tf_op jit(solution)/shard_map/doc_top/pallas_call | solution.py:572
  115.8 16.0 %ffn_grads.1 = (bf16[512,2048]{1,0:T(8,128)(2,1)}, bf16[512,2048]{1,0:T(8,128)(2,1)}, bf16[4,2,2,384,256]{4,3,2,1,0:T(8,128)(2,1)}, bf16[4,2,2,384,256]{4,3,2,1,0:T(8,128)(2,1)}) custom-call(s32[1]{0:T(128)} %bitcast.3.own, bf16[512,768]{1,0:T(8,128)(2,1)} %get-tuple-element.145.d_ffn, bf16[512,768]{1,0:T(8,128)(2,1)} %get-tuple-element.146.n2_d, ...), custom_call_target="tpu_custom_call" | custom-call | flops 999999995904 | bytes 1 | tf_op jit(solution)/shard_map/ffn_grads/pallas_call | solution.py:652
  132.3 4.0 %near_down.1 = (bf16[4,2,112,256]{3,2,1,0:T(8,128)(2,1)}, bf16[4,2,112,256]{3,2,1,0:T(8,128)(2,1)}, bf16[4,2,112,256]{3,2,1,0:T(8,128)(2,1)}, bf16[4,2,112,256]{3,2,1,0:T(8,128)(2,1)}) custom-call(s32[4]{0:T(128)} %pad_add_fusion.me, bf16[4,2,2,224,256]{4,3,2,1,0:T(8,128)(2,1)} %get-tuple-element.156.keep, ...), custom_call_target="tpu_custom_call" | custom-call | flops 1 | bytes 1 | tf_op jit(solution)/shard_map/near_down/pallas_call | solution.py:1098
  139.4 13.3 %middle_back.1 = (f32[512,768]{1,0:T(8,128)}, f32[8,768]{1,0:T(8,128)}, bf16[768,768]{1,0:T(8,128)(2,1)}, bf16[768,768]{1,0:T(8,128)(2,1)}) custom-call(f32[512,768]{1,0:T(8,128)} %get-tuple-element.142.d_h2, f32[512,768]{1,0:T(8,128)} %get-tuple-element.143.hid, f32[256,768]{1,0:T(8,128)} %get-tuple-element.144.d_hid_q, ...), custom_call_target="tpu_custom_call" | custom-call | flops 999999995904 | bytes 1 | tf_op jit(solution)/shard_map/middle_back/pallas_call | solution.py:727
  152.6 5.0 %near_ffn.1 = (bf16[4,2,192,256]{3,2,1,0:T(8,128)(2,1)}, bf16[4,2,192,256]{3,2,1,0:T(8,128)(2,1)}, bf16[4,2,192,256]{3,2,1,0:T(8,128)(2,1)}, bf16[4,2,192,256]{3,2,1,0:T(8,128)(2,1)}) custom-call(s32[4]{0:T(128)} %pad_add_fusion.me, bf16[4,2,2,384,256]{4,3,2,1,0:T(8,128)(2,1)} %get-tuple-element.177.keep, ...), custom_call_target="tpu_custom_call" | custom-call | flops 1 | bytes 1 | tf_op jit(solution)/shard_map/near_ffn/pallas_call | solution.py:1098
  157.7 2.4 line_down.1
  161.8 2.4 collective-permute-start.21
  165.5 33.8 %attn_back.1 = (bf16[768,768]{1,0:T(8,128)(2,1)}, bf16[768,768]{1,0:T(8,128)(2,1)}, bf16[768,768]{1,0:T(8,128)(2,1)}, f32[16,32]{1,0:T(8,128)}, bf16[4,2,2,288,2...) custom-call(s32[1]{0:T(128)} %bitcast.3.own, f32[32,1024]{1,0:T(8,128)} %constant.60.clone.hot, ...), custom_call_target="tpu_custom_call" | custom-call | flops 999999995904 | bytes 1 | tf_op jit(solution)/shard_map/attn_back/pallas_call | solution.py:891
  204.5 3.4 %line_ffn.1 = (bf16[2,2,192,256]{3,2,1,0:T(8,128)(2,1)}, bf16[2,2,192,256]{3,2,1,0:T(8,128)(2,1)}, bf16[2,2,192,256]{3,2,1,0:T(8,128)(2,1)}, bf16[2,2,192,256]{3,2,1,0:T(8,128)(2,1)}) custom-call(s32[4]{0:T(128)} %pad_add_fusion.me, bf16[4,2,192,256]{3,2,1,0:T(8,128)(2,1)} %get-tuple-element.179.refs_0_.a, ...), custom_call_target="tpu_custom_call" | custom-call | flops 1 | bytes 1 | tf_op jit(solution)/shard_map/line_ffn/pallas_call | solution.py:1113
  207.9 8.9 %input_back.1 = (bf16[512,768]{1,0:T(8,128)(2,1)}, bf16[256,768]{1,0:T(8,128)(2,1)}, f32[48,128]{1,0:T(8,128)}) custom-call(bf16[512,768]{1,0:T(8,128)(2,1)} %tok_d.1, bf16[256,768]{1,0:T(8,128)(2,1)} %tok_q.1, f32[512,768]{1,0:T(8,128)} %get-tuple-element.159.d_hid_d, f32[256,768]{1,0:T(8,128)} %get-tuple-element.144.d_hid_q, ...), custom_call_target="tpu_custom_call" | custom-call | flops 999999995904 | bytes 1 | tf_op jit(solution)/shard_map/input_back/pallas_call | solution.py:955
  216.8 4.6 %near_attn.1 = (bf16[4,2,144,256]{3,2,1,0:T(8,128)(2,1)}, bf16[4,2,144,256]{3,2,1,0:T(8,128)(2,1)}, bf16[4,2,144,256]{3,2,1,0:T(8,128)(2,1)}, bf16[4,2,144,256]{3,2,1,0:T(8,128)(2,1)}) custom-call(s32[4]{0:T(128)} %pad_add_fusion.me, bf16[4,2,2,288,256]{4,3,2,1,0:T(8,128)(2,1)} %get-tuple-element.199.keep, ...), custom_call_target="tpu_custom_call" | custom-call | flops 1 | bytes 1 | tf_op jit(solution)/shard_map/near_attn/pallas_call | solution.py:1098
  223.4 3.3 collective-permute-start.31
  228.7 13.8 %collective-permute-done.30.one = bf16[2,2,192,256]{3,2,1,0:T(8,128)(2,1)S(1)} collective-permute-done((bf16[2,2,192,256]{3,2,1,0:T(8,128)(2,1)}, bf16[2,2,192,256]{3,2,1,0:T(8,128)(2,1)S(1)}, u32[]{:S(2)}, u32[]{:S(2)}) %collective-permute-start.30) | collective-permute-done | bytes 393248 | tf_op jit(solution)/shard_map/ppermute | solution.py:1014
  242.5 2.4 collective-permute-start.29
  245.0 8.6 %collective-permute-done.31.two = bf16[2,2,192,256]{3,2,1,0:T(8,128)(2,1)S(1)} collective-permute-done((bf16[2,2,192,256]{3,2,1,0:T(8,128)(2,1)S(1)}, bf16[2,2,192,256]{3,2,1,0:T(8,128)(2,1)S(1)}, u32[]{:S(2)}, u32[]{:S(2)}) %collective-permute-start.31) | collective-permute-done | bytes 393248 | tf_op jit(solution)/shard_map/ppermute | solution.py:1014
  259.4 2.2 far_ffn.1
  265.0 2.4 collective-permute-start.42
  267.4 3.4 %collective-permute-done.42.three = f32[48,128]{1,0:T(8,128)S(1)} collective-permute-done((f32[48,128]{1,0:T(8,128)}, f32[48,128]{1,0:T(8,128)S(1)}, u32[]{:S(2)}, u32[]{:S(2)}) %collective-permute-start.42) | collective-permute-done | bytes 24608 | tf_op jit(solution)/shard_map/ppermute | solution.py:1014
  270.8 5.3 %collective-permute-start.41 = (f32[48,128]{1,0:T(8,128)}, f32[48,128]{1,0:T(8,128)S(1)}, u32[]{:S(2)}, u32[]{:S(2)}) collective-permute-start(f32[48,128]{1,0:T(8,128)} %sum_four.2.refs_0_.own), channel_id=1, source_target_pairs={{0,4},{1,5},{2,6},{3,7},{4,0},{5,1},{6,2},{7,3},{8,12},{9,13},{10,... | collective-permute-start | bytes 73736 | tf_op jit(solution)/shard_map/ppermute | solution.py:1014
  282.5 2.7 line_attn.1
  285.4 2.6 collective-permute-start.36
  301.6 4.9 %collective-permute-done.36.two = bf16[2,2,144,256]{3,2,1,0:T(8,128)(2,1)S(1)} collective-permute-done((bf16[2,2,144,256]{3,2,1,0:T(8,128)(2,1)}, bf16[2,2,144,256]{3,2,1,0:T(8,128)(2,1)S(1)}, u32[]{:S(2)}, u32[]{:S(2)}) %collective-permute-start.36) | collective-permute-done | bytes 294944 | tf_op jit(solution)/shard_map/ppermute | solution.py:1014
  313.3 2.5 unpack_ffn.1
  326.0 2.2 unpack_attn.1
  (183 shorter events, 78.9 us)
Async XLA Ops:
  34.8 38.7 %collective-permute-start.3 = (bf16[512,128]{1,0:T(8,128)(2,1)}, bf16[512,128]{1,0:T(8,128)(2,1)}, u32[]{:S(2)}, u32[]{:S(2)}) collective-permute-start(bf16[512,128]{1,0:T(8,128)(2,1)} %get-tuple-element.107.refs_0_.demb), channel_id=1, source_target_pairs={{0,1},{1,0},{2,3},{3,2},{4,5},{5,4},{6,7},{7,6},{8,9},{9,8},{10,11... | collective-permute-start | bytes 393224 | tf_op jit(solution)/shard_map/ppermute | solution.py:1014
  35.3 14.9 %collective-permute-start.2 = (bf16[512,128]{1,0:T(8,128)(2,1)}, bf16[512,128]{1,0:T(8,128)(2,1)}, u32[]{:S(2)}, u32[]{:S(2)}) collective-permute-start(bf16[512,128]{1,0:T(8,128)(2,1)} %get-tuple-element.107.refs_0_.demb), channel_id=1, source_target_pairs={{0,6},{1,7},{2,4},{3,5},{4,2},{5,3},{6,0},{7,1},{8,14},{9,15},{10,... | collective-permute-start | bytes 393224 | tf_op jit(solution)/shard_map/ppermute | solution.py:1014
  50.2 25.8 %collective-permute-start.6 = (bf16[512,128]{1,0:T(8,128)(2,1)}, bf16[512,128]{1,0:T(8,128)(2,1)}, u32[]{:S(2)}, u32[]{:S(2)}) collective-permute-start(bf16[512,128]{1,0:T(8,128)(2,1)} %collective-permute-done.2.refs_3_), channel_id=1, source_target_pairs={{0,1},{1,0},{2,3},{3,2},{4,5},{5,4},{6,7},{7,6},{8,9},{9,8},{10,11... | collective-permute-start | bytes 393224 | tf_op jit(solution)/shard_map/ppermute | solution.py:1014
  52.8 23.2 %collective-permute-start.5 = (bf16[512,128]{1,0:T(8,128)(2,1)}, bf16[512,128]{1,0:T(8,128)(2,1)}, u32[]{:S(2)}, u32[]{:S(2)}) collective-permute-start(bf16[512,128]{1,0:T(8,128)(2,1)} %collective-permute-done.1.refs_2_), channel_id=1, source_target_pairs={{0,1},{1,0},{2,3},{3,2},{4,5},{5,4},{6,7},{7,6},{8,9},{9,8},{10,11... | collective-permute-start | bytes 393224 | tf_op jit(solution)/shard_map/ppermute | solution.py:1014
  52.8 25.2 %collective-permute-start.4 = (bf16[512,128]{1,0:T(8,128)(2,1)}, bf16[512,128]{1,0:T(8,128)(2,1)}, u32[]{:S(2)}, u32[]{:S(2)}) collective-permute-start(bf16[512,128]{1,0:T(8,128)(2,1)} %collective-permute-done.refs_1_), channel_id=1, source_target_pairs={{0,1},{1,0},{2,3},{3,2},{4,5},{5,4},{6,7},{7,6},{8,9},{9,8},{10,11... | collective-permute-start | bytes 393224 | tf_op jit(solution)/shard_map/ppermute | solution.py:1014
  73.4 28.2 %collective-permute-start.10 = (bf16[256,128]{1,0:T(8,128)(2,1)}, bf16[256,128]{1,0:T(8,128)(2,1)}, u32[]{:S(2)}, u32[]{:S(2)}) collective-permute-start(bf16[256,128]{1,0:T(8,128)(2,1)} %get-tuple-element.108.qemb.refs_0_), channel_id=1, source_target_pairs={{0,1},{1,0},{2,3},{3,2},{4,5},{5,4},{6,7},{7,6},{8,9},{9,8},{10,11... | collective-permute-start | bytes 196616 | tf_op jit(solution)/shard_map/ppermute | solution.py:1014
  83.4 17.0 %all-to-all-start.1 = ((f32[8,1,256]{2,1,0:T(1,128)}), f32[8,1,256]{2,1,0:T(1,128)}, u32[]{:S(2)}, u32[]{:S(2)}) async-start(f32[8,1,256]{2,1,0:T(1,128)} %copy.46), calls=%async_computation.1 | async-start | bytes 16384 | tf_op jit(solution)/shard_map/all_to_all | solution.py:1223
  87.4 14.3 %collective-permute-start.13 = (bf16[256,128]{1,0:T(8,128)(2,1)}, bf16[256,128]{1,0:T(8,128)(2,1)}, u32[]{:S(2)}, u32[]{:S(2)}) collective-permute-start(bf16[256,128]{1,0:T(8,128)(2,1)} %collective-permute-done.9.refs_3_), channel_id=1, source_target_pairs={{0,1},{1,0},{2,3},{3,2},{4,5},{5,4},{6,7},{7,6},{8,9},{9,8},{10,11... | collective-permute-start | bytes 196616 | tf_op jit(solution)/shard_map/ppermute | solution.py:1014
  115.6 16.7 %collective-permute-start.14 = (bf16[4,2,2,224,256]{4,3,2,1,0:T(8,128)(2,1)}, bf16[4,2,2,224,256]{4,3,2,1,0:T(8,128)(2,1)}, u32[]{:S(2)}, u32[]{:S(2)}) collective-permute-start(bf16[4,2,2,224,256]{4,3,2,1,0:T(8,128)(2,1)} %get-tuple-element.157), channel_id=1, source_target_pairs={{0,1},{1,0},{2,3},{3,2},{4,5},{5,4},{6,7},{7,6},{8,9},{9,8},{10,11... | collective-permute-start | bytes 5505032 | tf_op jit(solution)/shard_map/ppermute | solution.py:1014
  131.8 20.8 %collective-permute-start.17 = (bf16[4,2,2,384,256]{4,3,2,1,0:T(8,128)(2,1)}, bf16[4,2,2,384,256]{4,3,2,1,0:T(8,128)(2,1)}, u32[]{:S(2)}, u32[]{:S(2)}) collective-permute-start(bf16[4,2,2,384,256]{4,3,2,1,0:T(8,128)(2,1)} %get-tuple-element.178), channel_id=1, source_target_pairs={{0,1},{1,0},{2,3},{3,2},{4,5},{5,4},{6,7},{7,6},{8,9},{9,8},{10,11... | collective-permute-start | bytes 9437192 | tf_op jit(solution)/shard_map/ppermute | solution.py:1014
  136.3 21.3 %collective-permute-start.15 = (bf16[4,2,112,256]{3,2,1,0:T(8,128)(2,1)}, bf16[4,2,112,256]{3,2,1,0:T(8,128)(2,1)}, u32[]{:S(2)}, u32[]{:S(2)}) collective-permute-start(bf16[4,2,112,256]{3,2,1,0:T(8,128)(2,1)} %get-tuple-element.174), channel_id=1, source_target_pairs={{0,8},{8,0},{16,24},{24,16},{1,9},{9,1},{17,25},{25,17},{2,10},{10... | collective-permute-start | bytes 1376264 | tf_op jit(solution)/shard_map/ppermute | solution.py:1014
  137.8 19.8 %collective-permute-start.16 = (bf16[4,2,112,256]{3,2,1,0:T(8,128)(2,1)}, bf16[4,2,112,256]{3,2,1,0:T(8,128)(2,1)}, u32[]{:S(2)}, u32[]{:S(2)}) collective-permute-start(bf16[4,2,112,256]{3,2,1,0:T(8,128)(2,1)} %get-tuple-element.176), channel_id=1, source_target_pairs={{0,16},{8,24},{16,0},{24,8},{1,17},{9,25},{17,1},{25,9},{2,18},{10... | collective-permute-start | bytes 1376264 | tf_op jit(solution)/shard_map/ppermute | solution.py:1014
  160.1 39.2 %collective-permute-start.20 = (bf16[2,2,112,256]{3,2,1,0:T(8,128)(2,1)}, bf16[2,2,112,256]{3,2,1,0:T(8,128)(2,1)}, u32[]{:S(2)}, u32[]{:S(2)}) collective-permute-start(bf16[2,2,112,256]{3,2,1,0:T(8,128)(2,1)} %get-tuple-element.192), channel_id=1, source_target_pairs={{0,2},{1,3},{2,0},{3,1},{4,6},{5,7},{6,4},{7,5},{8,10},{9,11},{10,... | collective-permute-start | bytes 688136 | tf_op jit(solution)/shard_map/ppermute | solution.py:1014
  161.8 37.6 %collective-permute-start.21 = (bf16[2,2,112,256]{3,2,1,0:T(8,128)(2,1)}, bf16[2,2,112,256]{3,2,1,0:T(8,128)(2,1)}, u32[]{:S(2)}, u32[]{:S(2)}) collective-permute-start(bf16[2,2,112,256]{3,2,1,0:T(8,128)(2,1)} %get-tuple-element.193), channel_id=1, source_target_pairs={{0,4},{1,5},{2,6},{3,7},{4,0},{5,1},{6,2},{7,3},{8,12},{9,13},{10,... | collective-permute-start | bytes 688136 | tf_op jit(solution)/shard_map/ppermute | solution.py:1014
  164.1 35.3 %collective-permute-start.22 = (bf16[2,2,112,256]{3,2,1,0:T(8,128)(2,1)}, bf16[2,2,112,256]{3,2,1,0:T(8,128)(2,1)}, u32[]{:S(2)}, u32[]{:S(2)}) collective-permute-start(bf16[2,2,112,256]{3,2,1,0:T(8,128)(2,1)} %get-tuple-element.194), channel_id=1, source_target_pairs={{0,6},{1,7},{2,4},{3,5},{4,2},{5,3},{6,0},{7,1},{8,14},{9,15},{10,... | collective-permute-start | bytes 688136 | tf_op jit(solution)/shard_map/ppermute | solution.py:1014
  164.5 40.0 %collective-permute-start.18 = (bf16[4,2,192,256]{3,2,1,0:T(8,128)(2,1)}, bf16[4,2,192,256]{3,2,1,0:T(8,128)(2,1)}, u32[]{:S(2)}, u32[]{:S(2)}) collective-permute-start(bf16[4,2,192,256]{3,2,1,0:T(8,128)(2,1)} %get-tuple-element.189), channel_id=1, source_target_pairs={{0,8},{8,0},{16,24},{24,16},{1,9},{9,1},{17,25},{25,17},{2,10},{10... | collective-permute-start | bytes 2359304 | tf_op jit(solution)/shard_map/ppermute | solution.py:1014
  165.0 39.5 %collective-permute-start.19 = (bf16[4,2,192,256]{3,2,1,0:T(8,128)(2,1)}, bf16[4,2,192,256]{3,2,1,0:T(8,128)(2,1)}, u32[]{:S(2)}, u32[]{:S(2)}) collective-permute-start(bf16[4,2,192,256]{3,2,1,0:T(8,128)(2,1)} %get-tuple-element.191), channel_id=1, source_target_pairs={{0,16},{8,24},{16,0},{24,8},{1,17},{9,25},{17,1},{25,9},{2,18},{10... | collective-permute-start | bytes 2359304 | tf_op jit(solution)/shard_map/ppermute | solution.py:1014
  199.3 17.5 %collective-permute-start.23 = (bf16[4,2,2,288,256]{4,3,2,1,0:T(8,128)(2,1)}, bf16[4,2,2,288,256]{4,3,2,1,0:T(8,128)(2,1)}, u32[]{:S(2)}, u32[]{:S(2)}) collective-permute-start(bf16[4,2,2,288,256]{4,3,2,1,0:T(8,128)(2,1)} %get-tuple-element.200), channel_id=1, source_target_pairs={{0,1},{1,0},{2,3},{3,2},{4,5},{5,4},{6,7},{7,6},{8,9},{9,8},{10,11... | collective-permute-start | bytes 7077896 | tf_op jit(solution)/shard_map/ppermute | solution.py:1014
  201.5 21.1 %collective-permute-start.34 = (bf16[2,112,256]{2,1,0:T(8,128)(2,1)}, bf16[2,112,256]{2,1,0:T(8,128)(2,1)}, u32[]{:S(2)}, u32[]{:S(2)}) collective-permute-start(bf16[2,112,256]{2,1,0:T(8,128)(2,1)} %get-tuple-element.209.b), channel_id=1, source_target_pairs={{0,8},{8,0},{16,24},{24,16},{1,9},{9,1},{17,25},{25,17},{2,10},{10... | collective-permute-start | bytes 344072 | tf_op jit(solution)/shard_map/ppermute | solution.py:1014
  202.9 20.5 %collective-permute-start.33 = (bf16[2,112,256]{2,1,0:T(8,128)(2,1)}, bf16[2,112,256]{2,1,0:T(8,128)(2,1)}, u32[]{:S(2)}, u32[]{:S(2)}) collective-permute-start(bf16[2,112,256]{2,1,0:T(8,128)(2,1)} %get-tuple-element.195.refs_0_.a), channel_id=1, source_target_pairs={{0,16},{8,24},{16,0},{24,8},{1,17},{9,25},{17,1},{25,9},{2,18},{10... | collective-permute-start | bytes 344072 | tf_op jit(solution)/shard_map/ppermute | solution.py:1014
  221.5 58.7 %collective-permute-start.24 = (bf16[4,2,144,256]{3,2,1,0:T(8,128)(2,1)}, bf16[4,2,144,256]{3,2,1,0:T(8,128)(2,1)S(1)}, u32[]{:S(2)}, u32[]{:S(2)}) collective-permute-start(bf16[4,2,144,256]{3,2,1,0:T(8,128)(2,1)} %get-tuple-element.203), channel_id=1, source_target_pairs={{0,8},{8,0},{16,24},{24,16},{1,9},{9,1},{17,25},{25,17},{2,10},{10... | collective-permute-start | bytes 1769480 | tf_op jit(solution)/shard_map/ppermute | solution.py:1014
  222.1 59.6 %collective-permute-start.25 = (bf16[4,2,144,256]{3,2,1,0:T(8,128)(2,1)}, bf16[4,2,144,256]{3,2,1,0:T(8,128)(2,1)S(1)}, u32[]{:S(2)}, u32[]{:S(2)}) collective-permute-start(bf16[4,2,144,256]{3,2,1,0:T(8,128)(2,1)} %get-tuple-element.205), channel_id=1, source_target_pairs={{0,16},{8,24},{16,0},{24,8},{1,17},{9,25},{17,1},{25,9},{2,18},{10... | collective-permute-start | bytes 1769480 | tf_op jit(solution)/shard_map/ppermute | solution.py:1014
  222.6 19.9 %collective-permute-start.30 = (bf16[2,2,192,256]{3,2,1,0:T(8,128)(2,1)}, bf16[2,2,192,256]{3,2,1,0:T(8,128)(2,1)S(1)}, u32[]{:S(2)}, u32[]{:S(2)}) collective-permute-start(bf16[2,2,192,256]{3,2,1,0:T(8,128)(2,1)} %get-tuple-element.206), channel_id=1, source_target_pairs={{0,2},{1,3},{2,0},{3,1},{4,6},{5,7},{6,4},{7,5},{8,10},{9,11},{10,... | collective-permute-start | bytes 1179656 | tf_op jit(solution)/shard_map/ppermute | solution.py:1014
  223.4 30.1 %collective-permute-start.31 = (bf16[2,2,192,256]{3,2,1,0:T(8,128)(2,1)S(1)}, bf16[2,2,192,256]{3,2,1,0:T(8,128)(2,1)S(1)}, u32[]{:S(2)}, u32[]{:S(2)}) collective-permute-start(bf16[2,2,192,256]{3,2,1,0:T(8,128)(2,1)S(1)} %copy-done.32), channel_id=1, source_target_pairs={{0,4},{1,5},{2,6},{3,7},{4,0},{5,1},{6,2},{7,3},{8,12},{9,13},{10,... | collective-permute-start | bytes 1179656 | tf_op jit(solution)/shard_map/ppermute | solution.py:1014
  226.7 30.1 %collective-permute-start.32 = (bf16[2,2,192,256]{3,2,1,0:T(8,128)(2,1)S(1)}, bf16[2,2,192,256]{3,2,1,0:T(8,128)(2,1)S(1)}, u32[]{:S(2)}, u32[]{:S(2)}) collective-permute-start(bf16[2,2,192,256]{3,2,1,0:T(8,128)(2,1)S(1)} %copy-done.31), channel_id=1, source_target_pairs={{0,6},{1,7},{2,4},{3,5},{4,2},{5,3},{6,0},{7,1},{8,14},{9,15},{10,... | collective-permute-start | bytes 1179656 | tf_op jit(solution)/shard_map/ppermute | solution.py:1014
  242.5 14.9 %collective-permute-start.29 = (f32[48,128]{1,0:T(8,128)}, f32[48,128]{1,0:T(8,128)S(1)}, u32[]{:S(2)}, u32[]{:S(2)}) collective-permute-start(f32[48,128]{1,0:T(8,128)} %sum_two.1.refs_0_.own), channel_id=1, source_target_pairs={{0,24},{8,16},{16,8},{24,0},{1,25},{9,17},{17,9},{25,1},{2,26},{10... | collective-permute-start | bytes 73736 | tf_op jit(solution)/shard_map/ppermute | solution.py:1014
  256.8 28.5 %collective-permute-start.44 = (bf16[2,112,256]{2,1,0:T(8,128)(2,1)}, bf16[2,112,256]{2,1,0:T(8,128)(2,1)S(1)}, u32[]{:S(2)}, u32[]{:S(2)}) collective-permute-start(bf16[2,112,256]{2,1,0:T(8,128)(2,1)} %get-tuple-element.217.b_own), channel_id=1, source_target_pairs={{0,16},{8,24},{16,0},{24,8},{1,17},{9,25},{17,1},{25,9},{2,18},{10... | collective-permute-start | bytes 344072 | tf_op jit(solution)/shard_map/ppermute | solution.py:1014
  257.4 30.6 %collective-permute-start.43 = (bf16[2,112,256]{2,1,0:T(8,128)(2,1)}, bf16[2,112,256]{2,1,0:T(8,128)(2,1)S(1)}, u32[]{:S(2)}, u32[]{:S(2)}) collective-permute-start(bf16[2,112,256]{2,1,0:T(8,128)(2,1)} %get-tuple-element.210.refs_0_.a_own), channel_id=1, source_target_pairs={{0,8},{8,0},{16,24},{24,16},{1,9},{9,1},{17,25},{25,17},{2,10},{10... | collective-permute-start | bytes 344072 | tf_op jit(solution)/shard_map/ppermute | solution.py:1014
  285.2 16.4 %collective-permute-start.35 = (bf16[2,2,144,256]{3,2,1,0:T(8,128)(2,1)}, bf16[2,2,144,256]{3,2,1,0:T(8,128)(2,1)S(1)}, u32[]{:S(2)}, u32[]{:S(2)}) collective-permute-start(bf16[2,2,144,256]{3,2,1,0:T(8,128)(2,1)} %get-tuple-element.213), channel_id=1, source_target_pairs={{0,2},{1,3},{2,0},{3,1},{4,6},{5,7},{6,4},{7,5},{8,10},{9,11},{10,... | collective-permute-start | bytes 884744 | tf_op jit(solution)/shard_map/ppermute | solution.py:1014
  285.4 21.2 %collective-permute-start.36 = (bf16[2,2,144,256]{3,2,1,0:T(8,128)(2,1)}, bf16[2,2,144,256]{3,2,1,0:T(8,128)(2,1)S(1)}, u32[]{:S(2)}, u32[]{:S(2)}) collective-permute-start(bf16[2,2,144,256]{3,2,1,0:T(8,128)(2,1)} %get-tuple-element.214), channel_id=1, source_target_pairs={{0,4},{1,5},{2,6},{3,7},{4,0},{5,1},{6,2},{7,3},{8,12},{9,13},{10,... | collective-permute-start | bytes 884744 | tf_op jit(solution)/shard_map/ppermute | solution.py:1014
  287.9 18.6 %collective-permute-start.37 = (bf16[2,2,144,256]{3,2,1,0:T(8,128)(2,1)}, bf16[2,2,144,256]{3,2,1,0:T(8,128)(2,1)S(1)}, u32[]{:S(2)}, u32[]{:S(2)}) collective-permute-start(bf16[2,2,144,256]{3,2,1,0:T(8,128)(2,1)} %get-tuple-element.215), channel_id=1, source_target_pairs={{0,6},{1,7},{2,4},{3,5},{4,2},{5,3},{6,0},{7,1},{8,14},{9,15},{10,... | collective-permute-start | bytes 884744 | tf_op jit(solution)/shard_map/ppermute | solution.py:1014
  296.5 15.4 %collective-permute-start.48 = (bf16[2,192,256]{2,1,0:T(8,128)(2,1)}, bf16[2,192,256]{2,1,0:T(8,128)(2,1)S(1)}, u32[]{:S(2)}, u32[]{:S(2)}) collective-permute-start(bf16[2,192,256]{2,1,0:T(8,128)(2,1)} %get-tuple-element.222.b_own), channel_id=1, source_target_pairs={{0,16},{8,24},{16,0},{24,8},{1,17},{9,25},{17,1},{25,9},{2,18},{10... | collective-permute-start | bytes 589832 | tf_op jit(solution)/shard_map/ppermute | solution.py:1014
  (54 other events, 464.9 us)
